TPU v7x, 32 devices: a whole 2x2x4 slice. The times are simulated.
32 devices in a mesh: cells: 8 (over z, y), rank: 4 (over x, core).
Axes of the slice: x: 2, y: 2, z: 4, core: 2. Of those that a mesh axis runs over, the one named last changes fastest.
Arguments:
- x_emb: bfloat16 [4096, 256], P('cells'), may hold values from -40 to 40, as said below
- y_emb: bfloat16 [4096, 256], P('cells'), may hold values from -40 to 40, as said below
- q_factor: float32 [4096, 512], P('cells', 'rank'), may hold values from 0 to 45, as said below
- r_factor: float32 [4096, 512], P('cells', 'rank'), may hold values from 0 to 45, as said below
- g_weights: float32 [512], P('rank'), may hold values from 2048 to 8192
- a_mass: float32 [4096], P('cells'), may hold values from 128 to 512
- b_mass: float32 [4096], P('cells'), may hold values from 128 to 512
- expr: bfloat16 [4096, 2048], P('cells', 'rank'), may hold values from -9 to 9, as said below
Outputs:
- q_new: float32 [4096, 512], P('cells', 'rank')
- r_new: float32 [4096, 512], P('cells', 'rank')
- rank_share: float32 [512], P('rank')
- predicted: bfloat16 [4096, 2048], P('cells', 'rank')
Inputs may be any that keep to these rules, and one draw needn't show every extreme that they name: `x_emb`: finite embedding values. `y_emb`: finite embedding values. `q_factor`: every entry is positive. `r_factor`: every entry is positive. `expr`: finite expression values.
All inputs are finite; a program needn't handle non-finite values. Where the computation divides by a largest or mean magnitude, that divisor is 1e-20 or more.
Results may differ from a plain program's by a relative error of at most 0.0075.
Values may be sent and summed in bfloat16 or wider, within the bound.
A program may use at most 64 MiB of HBM per device.

v0:
```python
import jax
import jax.numpy as jnp
from jax import lax
from jax.sharding import PartitionSpec as P

PASSES = 10


SCALE = 0.0625
GAMMA = 10.0
POWER = 0.8


def contract_rows(left, right):
    return lax.dot_general(
        left, right, (((0,), (0,)), ((), ())), preferred_element_type=jnp.float32
    )


def marginal_passes(kern_q, kern_r, kern_g, a_mass, b_mass, rows_total, columns_total):
    width = kern_q.shape[1]
    count = kern_q.shape[0]

    def one_pass(step, carry):
        v_q, v_r, weights, u_q, u_r = carry
        s_q, s_r = rows_total(
            jnp.sum(kern_q * v_q[None, :], axis=1), jnp.sum(kern_r * v_r[None, :], axis=1)
        )
        u_q = (a_mass / s_q) ** POWER
        u_r = (b_mass / s_r) ** POWER
        t_q, t_r = columns_total(
            jnp.sum(kern_q * u_q[:, None], axis=0), jnp.sum(kern_r * u_r[:, None], axis=0)
        )
        weights = jnp.exp((jnp.log(kern_g) + jnp.log(v_q * t_q) + jnp.log(v_r * t_r)) / 3.0)
        return (weights / t_q, weights / t_r, weights, u_q, u_r)

    start = (
        jnp.ones((width,), jnp.float32),
        jnp.ones((width,), jnp.float32),
        kern_g,
        jnp.ones((count,), jnp.float32),
        jnp.ones((count,), jnp.float32),
    )
    return lax.fori_loop(0, PASSES, one_pass, start)


def shards(x_emb, y_emb, q_factor, r_factor, g_weights, a_mass, b_mass, expr):
    local_rows = q_factor.shape[0]
    rank_local = q_factor.shape[1]
    cells_total = local_rows * lax.axis_size("cells")
    norms_one = jnp.sum(jnp.square(x_emb.astype(jnp.float32)), axis=1)
    norms_two = jnp.sum(jnp.square(y_emb.astype(jnp.float32)), axis=1)
    q_round = q_factor.astype(jnp.bfloat16)
    r_round = r_factor.astype(jnp.bfloat16)
    cross_xq, cross_yr, xq_vec, cq_vec, yr_vec, cr_vec = lax.psum(
        (
            contract_rows(x_emb, q_round),
            contract_rows(y_emb, r_round),
            jnp.sum(norms_one[:, None] * q_factor, axis=0),
            jnp.sum(q_factor, axis=0),
            jnp.sum(norms_two[:, None] * r_factor, axis=0),
            jnp.sum(r_factor, axis=0),
        ),
        "cells",
    )
    grad_q = (
        SCALE
        * (
            norms_one[:, None] * cr_vec[None, :]
            + yr_vec[None, :]
            - 2.0
            * jnp.dot(x_emb, cross_yr.astype(jnp.bfloat16), preferred_element_type=jnp.float32)
        )
        / g_weights[None, :]
    )
    grad_r = (
        SCALE
        * (
            norms_two[:, None] * cq_vec[None, :]
            + xq_vec[None, :]
            - 2.0
            * jnp.dot(y_emb, cross_xq.astype(jnp.bfloat16), preferred_element_type=jnp.float32)
        )
        / g_weights[None, :]
    )
    curvature = SCALE * (
        xq_vec * cr_vec + cq_vec * yr_vec - 2.0 * jnp.sum(cross_xq * cross_yr, axis=0)
    )
    grad_g = -curvature / jnp.square(g_weights)
    local_peak = jnp.maximum(
        jnp.max(jnp.abs(grad_q)), jnp.maximum(jnp.max(jnp.abs(grad_r)), jnp.max(jnp.abs(grad_g)))
    )
    peak = lax.pmax(local_peak, ("cells", "rank"))
    eta = GAMMA / (peak + 1e-06)
    kern_q = q_factor * jnp.exp(-eta * grad_q)
    kern_r = r_factor * jnp.exp(-eta * grad_r)
    kern_g = g_weights * jnp.exp(-eta * grad_g)
    whole_q, whole_r, whole_g = (
        lax.all_gather(kern_q.astype(jnp.bfloat16), "rank", axis=1, tiled=True).astype(
            kern_q.dtype
        ),
        lax.all_gather(kern_r.astype(jnp.bfloat16), "rank", axis=1, tiled=True).astype(
            kern_r.dtype
        ),
        lax.all_gather(kern_g.astype(jnp.bfloat16), "rank", axis=0, tiled=True).astype(
            kern_g.dtype
        ),
    )

    def keep_rows(first, second):
        return (first, second)

    def wide_columns(first, second):
        return lax.psum((first, second), "cells")

    v_q, v_r, weights, u_q, u_r = marginal_passes(
        whole_q, whole_r, whole_g, a_mass, b_mass, keep_rows, wide_columns
    )
    full_q = u_q[:, None] * whole_q * v_q[None, :]
    full_r = u_r[:, None] * whole_r * v_r[None, :]
    row_mass = jnp.sum(full_q, axis=1)
    scaled_all = (full_q / weights[None, :]).astype(jnp.bfloat16)
    right_all = full_r.astype(jnp.bfloat16)
    offset = lax.axis_index("rank") * rank_local
    q_new = lax.dynamic_slice_in_dim(full_q, offset, rank_local, 1)
    r_new = lax.dynamic_slice_in_dim(full_r, offset, rank_local, 1)
    weights_mine = lax.dynamic_slice_in_dim(weights, offset, rank_local, 0)
    profiles = lax.psum(contract_rows(right_all, expr), "cells")
    mixed = jnp.dot(scaled_all, profiles.astype(jnp.bfloat16), preferred_element_type=jnp.float32)
    predicted = (mixed / row_mass[:, None]).astype(jnp.bfloat16)
    return (q_new, r_new, weights_mine / cells_total, predicted)


def solution(mesh):
    return jax.shard_map(
        shards,
        mesh=mesh,
        in_specs=(
            P("cells", None),
            P("cells", None),
            P("cells", "rank"),
            P("cells", "rank"),
            P("rank"),
            P("cells"),
            P("cells"),
            P("cells", "rank"),
        ),
        out_specs=(P("cells", "rank"), P("cells", "rank"), P("rank"), P("cells", "rank")),
        check_vma=False,
    )
```

profile of v0, /device:TPU:0, one launch (start us, length us, event | category | flops | bytes accessed | tf_op | source)
XLA Modules:
  0.0 439.3 jit_solution(13786884739566823997)
XLA Ops:
  7.2 2.0 fusion.15
  9.3 0.9 fusion.13
  10.6 0.8 copy-done.3
  11.7 0.8 copy-done.6
  12.7 23.4 %all-reduce.1 = (f32[128]{0:T(128)S(1)}, f32[128]{0:T(128)S(1)}, f32[128]{0:T(128)S(1)}, f32[128]{0:T(128)S(1)}) all-reduce(f32[128]{0:T(128)S(1)} %get-tuple-element.237, f32[128]{0:T(128)S(1)} %reduce_sum.117, f32[128]{0:T(128)S(1)} %get-tuple-element.236, f32[128]{0:T(128)S(1)} %reduce_sum.120), channel_id=1, replica_groups=mesh['cells'=8,'rank'=4] {'cells'}, use_global_device_ids=true, to_apply=%region_5.0 | all-reduce | flops 512 | bytes 4096 | tf_op jit(solution)/shard_map/psum | solution.py:55
  36.1 49.5 %all-reduce.8.cloned.1.call-done = (f32[256,128]{1,0:T(8,128)}, f32[256,128]{1,0:T(8,128)}) async-done(((f32[256,128]{1,0:T(8,128)}, f32[256,128]{1,0:T(8,128)}), (f32[256,128]{1,0:T(8,128)}, f32[256,128]{1,0:T(8,128)})) %all-reduce.8.cloned.1.call-update) | async-done | bytes 262160 | tf_op jit(solution)/shard_map/psum | solution.py:55
  85.6 1.1 multiply_reduce_fusion.8
  86.7 0.6 copy-done.18
  87.3 0.8 abs_reduce_fusion.1
  88.2 0.8 abs_reduce_fusion
  89.1 0.6 abs_reduce_fusion.2
  91.6 39.6 %pmax.7 = f32[]{:T(128)} all-reduce(f32[]{:T(128)S(6)} %max.9), channel_id=1, replica_groups=mesh['cells'=8,'rank'=4] {'cells','rank'}, use_global_device_ids=true, to_apply=%region_16.0 | all-reduce | flops 1 | bytes 8 | tf_op jit(solution)/shard_map/pmax | solution.py:93
  132.0 5.3 %all-gather = bf16[4,1,128]{2,1,0:T(2,128)(2,1)S(1)} all-gather(bf16[1,1,128]{2,1,0:T(2,128)(2,1)S(1)} %convert_bitcast_fusion), channel_id=1, replica_groups=mesh['cells'=8,'rank'=4] {'rank'}, dimensions={0}, use_global_device_ids=true | all-gather | bytes 1280 | tf_op jit(solution)/shard_map/all_gather | solution.py:105
  137.3 7.7 %all_gather.10 = bf16[512,512]{0,1:T(8,128)(2,1)S(1)} all-gather(bf16[512,128]{0,1:T(8,128)(2,1)S(1)} %multiply_convert_fusion.1), channel_id=1, replica_groups=mesh['cells'=8,'rank'=4] {'rank'}, dimensions={1}, use_global_device_ids=true | all-gather | bytes 655360 | tf_op jit(solution)/shard_map/all_gather | solution.py:99
  145.3 0.6 copy-done.1
  145.9 7.3 %all_gather.11 = bf16[512,512]{0,1:T(8,128)(2,1)S(1)} all-gather(bf16[512,128]{0,1:T(8,128)(2,1)S(1)} %multiply_convert_fusion), channel_id=1, replica_groups=mesh['cells'=8,'rank'=4] {'rank'}, dimensions={1}, use_global_device_ids=true | all-gather | bytes 655360 | tf_op jit(solution)/shard_map/all_gather | solution.py:102
  153.4 0.5 copy-done.16
  153.9 202.5 %while.21 = (s32[]{:T(128)}, f32[512]{0:T(512)S(1)}, f32[512]{0:T(512)S(1)}, f32[512]{0:T(512)}, f32[512]{0:T(512)}, /*index=5*/f32[512]{0:T(512)}, f32[512,512]...) while((s32[]{:T(128)}, f32[512]{0:T(512)S(1)}, ...), condition=%wide.region_24.0_spmd.clone, body=%wide.region_17.0_spmd.clone.sunk | while | flops 2102787 | bytes 4284645 | solution.py:44
  154.3 0.4 copy-done.12
  154.9 0.3 copy-done.14
  155.2 20.6 %all-reduce.4 = (f32[512]{0:T(512)S(1)}, f32[512]{0:T(512)S(1)}) all-reduce(f32[512]{0:T(512)S(1)} %get-tuple-element.305, f32[512]{0:T(512)S(1)} %get-tuple-element.306), channel_id=1, replica_groups=mesh['cells'=8,'rank'=4] {'cells'}, use_global_device_ids=true, to_apply=%region_23.0 | all-reduce | flops 1024 | bytes 8192 | tf_op jit(solution)/shard_map/while/body/eval_jaxpr/psum | solution.py:114
  175.8 0.6 copy-done.10
  176.8 0.4 copy-done.12
  177.4 0.3 copy-done.14
  177.8 17.1 %all-reduce.4 = (f32[512]{0:T(512)S(1)}, f32[512]{0:T(512)S(1)}) all-reduce(f32[512]{0:T(512)S(1)} %get-tuple-element.305, f32[512]{0:T(512)S(1)} %get-tuple-element.306), channel_id=1, replica_groups=mesh['cells'=8,'rank'=4] {'cells'}, use_global_device_ids=true, to_apply=%region_23.0 | all-reduce | flops 1024 | bytes 8192 | tf_op jit(solution)/shard_map/while/body/eval_jaxpr/psum | solution.py:114
  194.9 0.6 copy-done.10
  195.9 0.4 copy-done.12
  196.5 0.3 copy-done.14
  196.8 19.1 %all-reduce.4 = (f32[512]{0:T(512)S(1)}, f32[512]{0:T(512)S(1)}) all-reduce(f32[512]{0:T(512)S(1)} %get-tuple-element.305, f32[512]{0:T(512)S(1)} %get-tuple-element.306), channel_id=1, replica_groups=mesh['cells'=8,'rank'=4] {'cells'}, use_global_device_ids=true, to_apply=%region_23.0 | all-reduce | flops 1024 | bytes 8192 | tf_op jit(solution)/shard_map/while/body/eval_jaxpr/psum | solution.py:114
  216.0 0.6 copy-done.10
  216.9 0.4 copy-done.12
  217.6 0.3 copy-done.14
  217.9 17.1 %all-reduce.4 = (f32[512]{0:T(512)S(1)}, f32[512]{0:T(512)S(1)}) all-reduce(f32[512]{0:T(512)S(1)} %get-tuple-element.305, f32[512]{0:T(512)S(1)} %get-tuple-element.306), channel_id=1, replica_groups=mesh['cells'=8,'rank'=4] {'cells'}, use_global_device_ids=true, to_apply=%region_23.0 | all-reduce | flops 1024 | bytes 8192 | tf_op jit(solution)/shard_map/while/body/eval_jaxpr/psum | solution.py:114
  235.1 0.6 copy-done.10
  236.0 0.4 copy-done.12
  236.7 0.3 copy-done.14
  237.0 19.1 %all-reduce.4 = (f32[512]{0:T(512)S(1)}, f32[512]{0:T(512)S(1)}) all-reduce(f32[512]{0:T(512)S(1)} %get-tuple-element.305, f32[512]{0:T(512)S(1)} %get-tuple-element.306), channel_id=1, replica_groups=mesh['cells'=8,'rank'=4] {'cells'}, use_global_device_ids=true, to_apply=%region_23.0 | all-reduce | flops 1024 | bytes 8192 | tf_op jit(solution)/shard_map/while/body/eval_jaxpr/psum | solution.py:114
  256.2 0.6 copy-done.10
  257.1 0.4 copy-done.12
  257.7 0.3 copy-done.14
  258.1 17.1 %all-reduce.4 = (f32[512]{0:T(512)S(1)}, f32[512]{0:T(512)S(1)}) all-reduce(f32[512]{0:T(512)S(1)} %get-tuple-element.305, f32[512]{0:T(512)S(1)} %get-tuple-element.306), channel_id=1, replica_groups=mesh['cells'=8,'rank'=4] {'cells'}, use_global_device_ids=true, to_apply=%region_23.0 | all-reduce | flops 1024 | bytes 8192 | tf_op jit(solution)/shard_map/while/body/eval_jaxpr/psum | solution.py:114
  275.2 0.6 copy-done.10
  276.2 0.4 copy-done.12
  276.8 0.3 copy-done.14
  277.2 19.1 %all-reduce.4 = (f32[512]{0:T(512)S(1)}, f32[512]{0:T(512)S(1)}) all-reduce(f32[512]{0:T(512)S(1)} %get-tuple-element.305, f32[512]{0:T(512)S(1)} %get-tuple-element.306), channel_id=1, replica_groups=mesh['cells'=8,'rank'=4] {'cells'}, use_global_device_ids=true, to_apply=%region_23.0 | all-reduce | flops 1024 | bytes 8192 | tf_op jit(solution)/shard_map/while/body/eval_jaxpr/psum | solution.py:114
  296.3 0.6 copy-done.10
  297.3 0.4 copy-done.12
  298.3 17.1 %all-reduce.4 = (f32[512]{0:T(512)S(1)}, f32[512]{0:T(512)S(1)}) all-reduce(f32[512]{0:T(512)S(1)} %get-tuple-element.305, f32[512]{0:T(512)S(1)} %get-tuple-element.306), channel_id=1, replica_groups=mesh['cells'=8,'rank'=4] {'cells'}, use_global_device_ids=true, to_apply=%region_23.0 | all-reduce | flops 1024 | bytes 8192 | tf_op jit(solution)/shard_map/while/body/eval_jaxpr/psum | solution.py:114
  315.4 0.6 copy-done.10
  316.4 0.4 copy-done.12
  317.3 19.1 %all-reduce.4 = (f32[512]{0:T(512)S(1)}, f32[512]{0:T(512)S(1)}) all-reduce(f32[512]{0:T(512)S(1)} %get-tuple-element.305, f32[512]{0:T(512)S(1)} %get-tuple-element.306), channel_id=1, replica_groups=mesh['cells'=8,'rank'=4] {'cells'}, use_global_device_ids=true, to_apply=%region_23.0 | all-reduce | flops 1024 | bytes 8192 | tf_op jit(solution)/shard_map/while/body/eval_jaxpr/psum | solution.py:114
  336.5 0.6 copy-done.10
  337.5 0.4 copy-done.12
  338.5 17.3 %all-reduce.4 = (f32[512]{0:T(512)S(1)}, f32[512]{0:T(512)S(1)}) all-reduce(f32[512]{0:T(512)S(1)} %get-tuple-element.305, f32[512]{0:T(512)S(1)} %get-tuple-element.306), channel_id=1, replica_groups=mesh['cells'=8,'rank'=4] {'cells'}, use_global_device_ids=true, to_apply=%region_23.0 | all-reduce | flops 1024 | bytes 8192 | tf_op jit(solution)/shard_map/while/body/eval_jaxpr/psum | solution.py:114
  355.8 0.6 copy-done.10
  356.4 0.7 copy-done.15
  357.1 1.3 fusion.19
  358.4 0.8 copy.26
  359.2 0.7 copy-done.13
  360.1 0.8 copy.27
  360.9 0.6 dynamic-slice_multiply_fusion
  361.5 0.5 fusion.10
  362.0 69.0 %all-reduce.9 = bf16[512,512]{1,0:T(8,128)(2,1)S(1)} all-reduce(f32[512,512]{1,0:T(8,128)S(1)} %fusion.10), channel_id=1, replica_groups=mesh['cells'=8,'rank'=4] {'cells'}, use_global_device_ids=true, to_apply=%region_25.0 | all-reduce | flops 262144 | bytes 1572864 | tf_op jit(solution)/shard_map/psum | solution.py:128
  431.0 1.5 fusion
  (171 shorter events, 8.7 us)
Async XLA Ops:
  7.2 354.3 %copy-start = (bf16[512,512]{1,0:T(8,128)(2,1)S(1)}, bf16[512,512]{1,0:T(8,128)(2,1)}, u32[]{:S(2)}) copy-start(bf16[512,512]{1,0:T(8,128)(2,1)} %param.17) | copy-start | bytes 1572868
  7.2 2.1 copy-start.5
  7.2 2.1 copy-start.4
  7.2 78.4 %all-reduce.8.cloned.1.call-start = ((), (), s32[]{:S(2)}) async-start(), calls=%async_computation | async-start | bytes 524288 | tf_op jit(solution)/shard_map/psum | solution.py:55
  10.4 1.0 copy-start.3
  11.5 1.0 copy-start.6
  85.6 1.1 copy-start.8
  86.7 0.7 copy-start.18
  87.3 0.9 copy-start.7
  137.3 8.6 %copy-start.9 = (f32[4,1,128]{2,1,0:T(1,128)}, f32[4,1,128]{2,1,0:T(1,128)S(1)}, u32[]{:S(2)}) copy-start(f32[4,1,128]{2,1,0:T(1,128)S(1)} %convert_element_type.64) | copy-start | bytes 6148
  145.0 0.8 copy-start.1
  153.2 0.7 copy-start.16
  153.2 0.7 copy-start.17
  154.1 0.6 copy-start.12
  154.7 0.6 copy-start.14
  175.8 0.6 copy-start.10
  176.6 0.6 copy-start.12
  177.2 0.6 copy-start.14
  194.9 0.6 copy-start.10
  195.7 0.6 copy-start.12
  196.3 0.6 copy-start.14
  216.0 0.6 copy-start.10
  216.8 0.6 copy-start.12
  217.3 0.6 copy-start.14
  235.1 0.6 copy-start.10
  235.8 0.6 copy-start.12
  236.4 0.6 copy-start.14
  256.1 0.6 copy-start.10
  256.9 0.6 copy-start.12
  257.5 0.6 copy-start.14
  275.2 0.6 copy-start.10
  276.0 0.6 copy-start.12
  276.6 0.6 copy-start.14
  296.3 0.6 copy-start.10
  297.1 0.6 copy-start.12
  297.7 0.6 copy-start.14
  315.4 0.6 copy-start.10
  316.2 0.6 copy-start.12
  316.8 0.6 copy-start.14
  336.5 0.6 copy-start.10
  337.3 0.6 copy-start.12
  337.9 0.6 copy-start.14
  355.8 0.6 copy-start.10
  356.4 0.7 copy-start.15
  359.2 0.7 copy-start.13
  360.1 0.8 copy-start.11
  362.0 69.0 %copy-start.2 = (bf16[512,512]{0,1:T(8,128)(2,1)S(1)}, bf16[512,512]{0,1:T(8,128)(2,1)}, u32[]{:S(2)}) copy-start(bf16[512,512]{0,1:T(8,128)(2,1)} %copy-done.1) | copy-start | bytes 1572868
Sparse Core Ops, SparseCore 0:
  12.1 73.5 all-reduce.7
where the time goes:
time: 440 us; the launch traced here: 439 us
  blocking collectives  335 us (76%)
  waiting for transfers between devices  49.6 us (11%)
  local copies, waits for them, and re-layouts  20.5 us (5%)
  between operations  16.9 us (4%)
  other arithmetic  10.2 us (2%)
  matrix products  6.57 us (1%)
    psum x10, blocking collectives, wide_columns(): return lax.psum((first, second), 'cells')  183 us
    psum x1, blocking collectives, shards(): profiles = lax.psum(contract_rows(right_all, expr), 'cells')  69 us
    psum x1, waiting for transfers between devices, shards(): lax.psum((contract_rows(x_emb, q_round), contract_rows(y_emb, r_round), j...  49.5 us
    pmax x1, blocking collectives, shards(): peak = lax.pmax(local_peak, ('cells', 'rank'))  39.6 us
    psum x1, blocking collectives, shards(): lax.psum((contract_rows(x_emb, q_round), contract_rows(y_emb, r_round), j...  23.4 us
    while x60, local copies, waits for them, and re-layouts  13.4 us
  transfers between devices with their start and end apart: 1, of which 1 were waited for; matrix products, arithmetic and copies ran while one was open for 0% of the time, Pallas kernels for 0%

commit v1 on v0

v1 whole, which is shorter than its diff:
```python
import functools

import jax
import jax.numpy as jnp
from jax import lax
from jax.experimental import pallas as pl
from jax.experimental.pallas import tpu as pltpu
from jax.sharding import PartitionSpec as P

PASSES = 10
SCALE = 0.0625
GAMMA = 10.0
POWER = 0.8
LANES = 128
MESH = pl.DeviceIdType.MESH
F32 = jnp.float32
BF16 = jnp.bfloat16


def dot(left, right):
    return jnp.dot(left, right, preferred_element_type=F32)


def contract_rows(left, right):
    return lax.dot_general(
        left, right, (((0,), (0,)), ((), ())), preferred_element_type=F32
    )


def wide(rows, first, count):
    return jnp.concatenate([rows[first + i : first + i + 1] for i in range(count)], axis=1)


def tall(*rows):
    return jnp.concatenate(
        [row[:, i * LANES : (i + 1) * LANES] for row in rows for i in range(row.shape[1] // LANES)],
        axis=0,
    )


def row_product(row, matrix):
    high = row.astype(BF16).astype(F32)
    low = row - high
    shape = (16, row.shape[1])
    index = lax.broadcasted_iota(jnp.int32, shape, 0)
    parts = jnp.where(
        index == 0,
        jnp.broadcast_to(high, shape),
        jnp.where(index == 1, jnp.broadcast_to(low, shape), 0.0),
    )
    out = dot(parts.astype(BF16), matrix)
    return out[0:1] + out[1:2]


def as_column(row):
    return jnp.transpose(jnp.broadcast_to(row, (LANES, row.shape[1])))


def pick_row(rows, index):
    position = lax.broadcasted_iota(jnp.int32, rows.shape, 0)
    return jnp.sum(jnp.where(position == index, rows, 0.0), axis=0, keepdims=True)


def kernel(
    n, ranks, owners, tiles, cells_total,
    x_ref, y_ref, q_ref, r_ref, g_ref, a_ref, b_ref, expr_ref,
    q_out, r_out, w_out, pred_out,
    factors, part_src, part_buf, cross, vec_buf, vecs, grads_q, grads_r, grads_g,
    peaks, kq, kr, kqt, krt, t_buf, prof_src, prof_buf, prof,
    part_send, part_recv, vec_send, vec_recv, cross_send, cross_recv,
    fac_send, fac_recv, rank_send, rank_recv, vr_send, vr_recv,
    peak_send, peak_recv, t_send, t_recv, prof_send, prof_recv, gat_send, gat_recv,
):
    me = lax.axis_index("cells")
    k = lax.axis_index("rank")
    near = k + 1 - 2 * lax.rem(k, 2)
    far = lax.rem(k + 2, 4)
    across = 3 - k

    def peers(body):
        if n <= 8:
            for offset in range(1, n):
                body(lax.rem(me + offset, n))
        else:
            def one(offset, carry):
                body(lax.rem(me + offset, n))
                return carry
            lax.fori_loop(1, n, one, 0)

    def only(limit, index, body):
        if limit >= n:
            body()
        else:
            pl.when(index < limit)(body)

    def to_peer(src, dst, send, recv, j):
        return pltpu.make_async_remote_copy(
            src_ref=src, dst_ref=dst, send_sem=send, recv_sem=recv,
            device_id=(j, k), device_id_type=MESH,
        )

    def to_rank(src, dst, send, recv, other):
        return pltpu.make_async_remote_copy(
            src_ref=src, dst_ref=dst, send_sem=send, recv_sem=recv,
            device_id=(me, other), device_id_type=MESH,
        )

    barrier = pltpu.get_barrier_semaphore()
    peers(lambda j: pl.semaphore_signal(barrier, inc=1, device_id=(j, k), device_id_type=MESH))
    for other in (near, far, across):
        pl.semaphore_signal(barrier, inc=1, device_id=(me, other), device_id_type=MESH)

    x, y = x_ref[...], y_ref[...]
    q, r = q_ref[...], r_ref[...]
    q_round, r_round = q.astype(BF16), r.astype(BF16)
    factors[k, 0] = q_round
    factors[k, 1] = r_round
    depth = part_src.shape[2]
    part_src[:, 0] = contract_rows(x, q_round).astype(BF16).reshape(owners, depth, LANES)
    part_src[:, 1] = contract_rows(y, r_round).astype(BF16).reshape(owners, depth, LANES)
    norms_one = jnp.sum(jnp.square(x.astype(F32)), axis=1, keepdims=True)
    norms_two = jnp.sum(jnp.square(y.astype(F32)), axis=1, keepdims=True)
    vec_buf[me] = jnp.concatenate(
        [
            jnp.sum(norms_one * q, axis=0, keepdims=True),
            jnp.sum(q, axis=0, keepdims=True),
            jnp.sum(norms_two * r, axis=0, keepdims=True),
            jnp.sum(r, axis=0, keepdims=True),
            jnp.zeros((4, LANES), F32),
        ],
        axis=0,
    )
    pl.semaphore_wait(barrier, n - 1 + 3)

    def part_copy(j, slot):
        return to_peer(part_src.at[lax.rem(j, owners)], part_buf.at[slot], part_send.at[j], part_recv.at[slot], j)

    def vec_copy(j, slot):
        return to_peer(vec_buf.at[me], vec_buf.at[slot], vec_send.at[j], vec_recv.at[slot], j)

    def send_parts(j):
        only(owners, j, lambda: part_copy(j, me).start())
        vec_copy(j, me).start()

    peers(send_parts)

    def factor_copy(slot, i, other):
        return to_rank(factors.at[slot], factors.at[slot], fac_send.at[i], fac_recv.at[i], other)

    factor_copy(k, 0, near).start()
    factor_copy(k, 1, far).start()

    def own_part():
        part_buf[me] = part_src[me]

    only(owners, me, own_part)

    def reduce_parts():
        peers(lambda j: part_copy(j, j).wait_recv())
        total = part_buf[0].astype(F32)
        for j in range(1, n):
            total = total + part_buf[j].astype(F32)
        cross[k, me] = total.astype(BF16)

    only(owners, me, reduce_parts)

    def cross_copy(j, slot):
        return to_peer(cross.at[k, slot], cross.at[k, slot], cross_send.at[j], cross_recv.at[slot], j)

    only(owners, me, lambda: peers(lambda j: cross_copy(j, me).start()))

    peers(lambda j: vec_copy(j, j).wait_recv())
    vec = vec_buf[0]
    for j in range(1, n):
        vec = vec + vec_buf[j]
    slot_row = lax.broadcasted_iota(jnp.int32, (8, LANES), 0)
    vecs[k] = jnp.where(slot_row == 4, jnp.broadcast_to(g_ref[...], (8, LANES)), vec)

    def vecs_copy(slot, i, other):
        return to_rank(vecs.at[slot], vecs.at[slot], vr_send.at[i], vr_recv.at[i], other)

    for i, other in enumerate((near, far, across)):
        vecs_copy(k, i, other).start()
    factor_copy(far, 1, far).wait_recv()
    factor_copy(far, 2, near).start()

    peers(lambda j: only(owners, j, lambda: cross_copy(j, j).wait_recv()))

    def rank_copy(slot, i, other):
        return to_rank(cross.at[slot], cross.at[slot], rank_send.at[i], rank_recv.at[i], other)

    rank_copy(k, 1, far).start()
    rank_copy(k, 0, near).start()

    def gradients(kk):
        info = vecs[kk]
        xq_vec, cq_vec, yr_vec, cr_vec, g = (info[i : i + 1] for i in range(5))
        scale = SCALE / g
        dim = x.shape[1]
        cross_xq = cross[kk, :, 0].reshape(dim, LANES)
        cross_yr = cross[kk, :, 1].reshape(dim, LANES)
        grad_q = (norms_one * cr_vec + yr_vec - 2.0 * dot(x, cross_yr)) * scale
        grad_r = (norms_two * cq_vec + xq_vec - 2.0 * dot(y, cross_xq)) * scale
        grads_q[kk] = grad_q
        grads_r[kk] = grad_r
        inner = jnp.sum(cross_xq.astype(F32) * cross_yr.astype(F32), axis=0, keepdims=True)
        curvature = SCALE * (xq_vec * cr_vec + cq_vec * yr_vec - 2.0 * inner)
        grad_g = -curvature / jnp.square(g)
        grads_g[kk] = jnp.broadcast_to(grad_g, (8, LANES))
        return jnp.maximum(
            jnp.max(jnp.maximum(jnp.abs(grad_q), jnp.abs(grad_r)), axis=0, keepdims=True),
            jnp.abs(grad_g),
        )

    peak = gradients(k)
    vecs_copy(near, 0, near).wait_recv()
    rank_copy(near, 0, near).wait_recv()
    peak = jnp.maximum(peak, gradients(near))
    rank_copy(far, 1, far).wait_recv()
    rank_copy(far, 2, near).start()
    vecs_copy(far, 1, far).wait_recv()
    peak = jnp.maximum(peak, gradients(far))
    vecs_copy(across, 2, across).wait_recv()
    rank_copy(across, 2, near).wait_recv()
    peak = jnp.maximum(peak, gradients(across))
    peaks[me] = jnp.broadcast_to(peak, (8, LANES))

    def peak_copy(j, slot):
        return to_peer(peaks.at[me], peaks.at[slot], peak_send.at[j], peak_recv.at[slot], j)

    peers(lambda j: peak_copy(j, me).start())
    factor_copy(near, 0, near).wait_recv()
    factor_copy(across, 2, near).wait_recv()
    log_a, log_b = jnp.log(a_ref[...]), jnp.log(b_ref[...])
    peers(lambda j: peak_copy(j, j).wait_recv())
    top = peaks[0]
    for j in range(1, n):
        top = jnp.maximum(top, peaks[j])
    eta = GAMMA / (jnp.max(top, axis=1, keepdims=True)[0:1] + 1e-6)

    log_g = []
    for kk in range(ranks):
        columns = slice(kk * LANES, (kk + 1) * LANES)
        kern_q = factors[kk, 0].astype(F32) * jnp.exp(-eta * grads_q[kk])
        kern_r = factors[kk, 1].astype(F32) * jnp.exp(-eta * grads_r[kk])
        kq[:, columns] = kern_q.astype(BF16)
        kr[:, columns] = kern_r.astype(BF16)
        kqt[columns, :] = jnp.transpose(kern_q).astype(BF16)
        krt[columns, :] = jnp.transpose(kern_r).astype(BF16)
        log_g.append(jnp.log(vecs[kk][4:5]) - eta * grads_g[kk][0:1])
    log_kern_g = jnp.concatenate(log_g + log_g, axis=0)

    def t_copy(parity, j, slot):
        return to_peer(
            t_buf.at[parity, me], t_buf.at[parity, slot],
            t_send.at[parity, j], t_recv.at[parity, slot], j,
        )

    def one_pass(step, carry):
        v, _, _, _, _ = carry
        parity = lax.rem(step, 2)
        s_q = row_product(wide(v, 0, ranks), kqt[...])
        s_r = row_product(wide(v, ranks, ranks), krt[...])
        u_q = jnp.exp(POWER * (log_a - jnp.log(s_q)))
        u_r = jnp.exp(POWER * (log_b - jnp.log(s_r)))
        t_buf[parity, me] = tall(row_product(u_q, kq[...]), row_product(u_r, kr[...]))
        peers(lambda j: t_copy(parity, j, me).start())
        peers(lambda j: t_copy(parity, j, j).wait_recv())
        t = t_buf[parity, 0]
        for j in range(1, n):
            t = t + t_buf[parity, j]
        peers(lambda j: t_copy(parity, j, j).wait_send())
        logs = jnp.log(v * t)
        other = jnp.concatenate([logs[ranks:], logs[:ranks]], axis=0)
        weights = jnp.exp((log_kern_g + logs + other) / 3.0)
        return weights / t, weights, t, u_q, u_r

    ones = jnp.ones((2 * ranks, LANES), F32)
    row = jnp.ones((1, x.shape[0]), F32)
    v, weights, t, u_q, u_r = lax.fori_loop(
        0, PASSES, one_pass, (ones, ones, ones, row, row)
    )

    share = prof_src.shape[1]
    left = (krt[...].astype(F32) * u_r).astype(BF16)
    prof_src[...] = dot(left, expr_ref[...]).astype(BF16).reshape(prof_src.shape)

    def prof_copy(j, slot):
        return to_peer(prof_src.at[lax.rem(j, tiles)], prof_buf.at[slot], prof_send.at[j], prof_recv.at[slot], j)

    peers(lambda j: only(tiles, j, lambda: prof_copy(j, me).start()))

    def own_prof():
        prof_buf[me] = prof_src[me]

    only(tiles, me, own_prof)

    w_out[...] = pick_row(weights, k) / cells_total
    own_q = q_ref[...] * jnp.exp(-eta * grads_q[k])
    own_r = r_ref[...] * jnp.exp(-eta * grads_r[k])
    q_out[...] = as_column(u_q) * own_q * pick_row(v, k)
    r_out[...] = as_column(u_r) * own_r * pick_row(v, k + ranks)
    inverse = as_column(1.0 / row_product(wide(v, 0, ranks), kqt[...]))
    scaled = (kq[...].astype(F32) * wide(v[ranks:] / t[:ranks], 0, ranks)).astype(BF16)

    def gather_copy(j, slot):
        return to_peer(prof.at[slot], prof.at[slot], gat_send.at[j], gat_recv.at[slot], j)

    def reduce_prof():
        peers(lambda j: prof_copy(j, j).wait_recv())
        total = prof_buf[0].astype(F32)
        for j in range(1, n):
            total = total + prof_buf[j].astype(F32)
        prof[me] = total.astype(BF16)
        peers(lambda j: gather_copy(j, me).start())

    only(tiles, me, reduce_prof)
    peers(lambda j: only(tiles, j, lambda: gather_copy(j, j).wait_recv()))
    mixed = dot(scaled, prof[...].reshape(tiles * share, prof.shape[2]))
    for i in range(mixed.shape[1] // LANES):
        columns = slice(i * LANES, (i + 1) * LANES)
        pred_out[:, columns] = (mixed[:, columns] * inverse).astype(BF16)

    def sends(j):
        only(owners, j, lambda: part_copy(j, j).wait_send())
        vec_copy(j, j).wait_send()
        only(owners, me, lambda: cross_copy(j, me).wait_send())
        peak_copy(j, j).wait_send()
        only(tiles, j, lambda: prof_copy(j, j).wait_send())
        only(tiles, me, lambda: gather_copy(j, me).wait_send())

    peers(sends)
    for i, (slot, other) in enumerate(((k, near), (k, far), (far, near))):
        factor_copy(slot, i, other).wait_send()
        rank_copy(slot, i, other).wait_send()
    for i, other in enumerate((near, far, across)):
        vecs_copy(k, i, other).wait_send()


def shards(n, ranks, x_emb, y_emb, q_factor, r_factor, g_weights, a_mass, b_mass, expr):
    rows, dim = x_emb.shape
    genes = expr.shape[1]
    rank_all = ranks * LANES
    owners = min(n, dim // 16)
    tiles = min(n, rank_all // 16)
    vmem = pl.BlockSpec(memory_space=pltpu.VMEM)
    dma = pltpu.SemaphoreType.DMA
    pair = [dma((n,)), dma((n,))]
    three = [dma((3,)), dma((3,))]
    q_new, r_new, rank_share, predicted = pl.pallas_call(
        functools.partial(kernel, n, ranks, owners, tiles, float(rows * n)),
        out_shape=(
            jax.ShapeDtypeStruct(q_factor.shape, F32),
            jax.ShapeDtypeStruct(r_factor.shape, F32),
            jax.ShapeDtypeStruct((1, LANES), F32),
            jax.ShapeDtypeStruct((rows, genes), BF16),
        ),
        in_specs=[vmem] * 8,
        out_specs=(vmem,) * 4,
        scratch_shapes=[
            pltpu.VMEM((ranks, 2, rows, LANES), BF16),
            pltpu.VMEM((owners, 2, dim // owners, LANES), BF16),
            pltpu.VMEM((n, 2, dim // owners, LANES), BF16),
            pltpu.VMEM((ranks, owners, 2, dim // owners, LANES), BF16),
            pltpu.VMEM((n, 8, LANES), F32),
            pltpu.VMEM((ranks, 8, LANES), F32),
            pltpu.VMEM((ranks, rows, LANES), F32),
            pltpu.VMEM((ranks, rows, LANES), F32),
            pltpu.VMEM((ranks, 8, LANES), F32),
            pltpu.VMEM((n, 8, LANES), F32),
            pltpu.VMEM((rows, rank_all), BF16),
            pltpu.VMEM((rows, rank_all), BF16),
            pltpu.VMEM((rank_all, rows), BF16),
            pltpu.VMEM((rank_all, rows), BF16),
            pltpu.VMEM((2, n, 8, LANES), F32),
            pltpu.VMEM((tiles, rank_all // tiles, genes), BF16),
            pltpu.VMEM((n, rank_all // tiles, genes), BF16),
            pltpu.VMEM((tiles, rank_all // tiles, genes), BF16),
        ]
        + pair + pair + pair + three + three + three + pair
        + [dma((2, n)), dma((2, n))]
        + pair + pair,
        compiler_params=pltpu.CompilerParams(
            collective_id=0, has_side_effects=True, vmem_limit_bytes=48 * 1024 * 1024
        ),
        cost_estimate=pl.CostEstimate(
            flops=2 * rows * (2 * dim * LANES + 2 * dim * rank_all + 2 * rank_all * genes),
            bytes_accessed=4 * 1024 * 1024,
            transcendentals=2 * rows * rank_all,
        ),
        name="transport_step",
    )(
        x_emb, y_emb, q_factor, r_factor, g_weights.reshape(1, LANES),
        a_mass.reshape(1, rows), b_mass.reshape(1, rows), expr,
    )
    return q_new, r_new, rank_share.reshape(LANES), predicted


def solution(mesh):
    n, ranks = mesh.shape["cells"], mesh.shape["rank"]
    assert ranks == 4
    return jax.shard_map(
        functools.partial(shards, n, ranks),
        mesh=mesh,
        in_specs=(
            P("cells", None),
            P("cells", None),
            P("cells", "rank"),
            P("cells", "rank"),
            P("rank"),
            P("cells"),
            P("cells"),
            P("cells", "rank"),
        ),
        out_specs=(P("cells", "rank"), P("cells", "rank"), P("rank"), P("cells", "rank")),
        check_vma=False,
    )
```

time: 440 us -> 100 us (0.23)
  blocking collectives: 335 us -> 0 us
  Pallas kernels: 0 us -> 91.3 us
  waiting for transfers between devices: 49.6 us -> 0 us
  between operations: 16.9 us -> 0.67 us
  local copies, waits for them, and re-layouts: 20.5 us -> 8.23 us
  other arithmetic: 10.2 us -> 0 us
  matrix products: 6.57 us -> 0 us
    psum x12 -> x0, blocking collectives: 275 us -> none  [the longest x10 183 us: wide_columns(): return lax.psum((first, second), 'cells')]
    pallas_call x0 -> x1, Pallas kernels: none -> 91.3 us  [shards(): pl.pallas_call(functools.partial(kernel, n, ranks, owners, tiles, float(r...]
    psum x1 -> x0, waiting for transfers between devices: 49.5 us -> none  [shards(): lax.psum((contract_rows(x_emb, q_round), contract_rows(y_emb, r_round), j...]
    pmax x1 -> x0, blocking collectives: 39.6 us -> none  [shards(): peak = lax.pmax(local_peak, ('cells', 'rank'))]
    all_gather x3 -> x0, blocking collectives: 20.3 us -> none  [the longest x1 7.71 us: shards(): lax.all_gather(kern_q.astype(jnp.bfloat16), 'rank', axis=1, tiled=True)]
    while x60 -> x0, local copies, waits for them, and re-layouts: 13.4 us -> none
    reduce_sum x37 -> x0, other arithmetic: 8.13 us -> none  [the longest x10 2.17 us: one_pass(): jnp.sum(kern_r * u_r[:, None], axis=0)]
    dot_general x6 -> x0, matrix products: 6.57 us -> none  [the longest x3 3.44 us: contract_rows(): lax.dot_general(left, right, (((0,), (0,)), ((), ())), preferred_element_...]
  transfers between devices with their start and end apart: 1 -> 0, of which waited for: 1 -> 0; matrix products, arithmetic and copies ran while one was open for 0% -> 0% of each run, Pallas kernels for 0% -> 0%
where the time goes in v1:
time: 100 us
  Pallas kernels  91.3 us (91%)
  local copies, waits for them, and re-layouts  8.23 us (8%)
    pallas_call x1, Pallas kernels, shards(): pl.pallas_call(functools.partial(kernel, n, ranks, owners, tiles, float(r...  91.3 us
    unnamed x20, local copies, waits for them, and re-layouts  8.23 us

profile of v1, /device:TPU:0, one launch (start us, length us, event | category | flops | bytes accessed | tf_op | source)
XLA Modules:
  0.0 100.2 jit_solution(8696439718509817333)
XLA Ops:
  0.6 0.0 copy-start.6
  0.6 0.0 copy-start.5
  0.7 0.0 copy-start.7
  0.7 0.7 copy-done.6
  1.3 0.0 copy-done.5
  1.3 0.0 copy-done.7
  1.3 0.0 copy-start
  1.3 1.0 %copy-done = bf16[512,512]{1,0:T(8,128)(2,1)S(1)} copy-done((bf16[512,512]{1,0:T(8,128)(2,1)S(1)}, bf16[512,512]{1,0:T(8,128)(2,1)}, u32[]{:S(2)}) %copy-start) | copy-done | bytes 524312
  2.4 0.0 copy-start.1
  2.4 0.9 copy-done.1
  3.3 0.0 copy-start.2
  3.3 0.9 copy-done.2
  4.3 0.0 copy-start.3
  4.3 0.9 copy-done.3
  5.2 0.0 copy-start.4
  5.2 0.9 copy-done.4
  6.2 91.3 %transport_step.1 = (f32[512,128]{1,0:T(8,128)S(1)}, f32[512,128]{1,0:T(8,128)S(1)}, f32[1,128]{1,0:T(1,128)S(1)}, bf16[512,512]{1,0:T(8,128)(2,1)S(1)}) custom-call(bf16[512,256]{1,0:T(8,128)(2,1)S(1)} %copy-done.1, bf16[512,256]{1,0:T(8,128)(2,1)S(1)} %copy-done.2, f32[512,128]{1,0:T(8,128)S(1)} %copy-done.3, f32[512,128]{1,0:T(8,128)S(1)} %copy-done.4, ...), custom_call_target="tpu_custom_call" | custom-call | flops 872415232 | bytes 4194304 | tf_op jit(solution)/shard_map/transport_step/pallas_call | solution.py:350
  97.4 0.7 copy.16
  98.1 0.7 copy.17
  98.9 0.5 copy.18
  99.4 0.8 copy.19
Async XLA Ops:
  0.6 0.7 copy-start.6
  0.6 0.7 copy-start.5
  0.7 0.7 copy-start.7
  1.3 1.0 %copy-start = (bf16[512,512]{1,0:T(8,128)(2,1)S(1)}, bf16[512,512]{1,0:T(8,128)(2,1)}, u32[]{:S(2)}) copy-start(bf16[512,512]{1,0:T(8,128)(2,1)} %expr_ref.1) | copy-start | bytes 1572868
  2.4 0.9 copy-start.1
  3.3 0.9 copy-start.2
  4.3 0.9 copy-start.3
  5.2 0.9 copy-start.4

commit v2 on v1

--- a/solution.py
+++ b/solution.py
@@ -12,6 +12,7 @@
 GAMMA = 10.0
 POWER = 0.8
 LANES = 128
+VMEM_LIMIT = 56 * 1024 * 1024
 MESH = pl.DeviceIdType.MESH
 F32 = jnp.float32
 BF16 = jnp.bfloat16
@@ -63,32 +64,45 @@
 
 def kernel(
     n, ranks, owners, tiles, cells_total,
-    x_ref, y_ref, q_ref, r_ref, g_ref, a_ref, b_ref, expr_ref,
-    q_out, r_out, w_out, pred_out,
+    x_hbm, y_hbm, q_hbm, r_hbm, g_hbm, a_hbm, b_hbm, expr_hbm,
+    q_hbm_out, r_hbm_out, w_hbm_out, pred_hbm_out,
+    q_out, r_out, w_out, pred_out, out_sem,
+    x_ref, y_ref, q_ref, r_ref, g_ref, a_ref, b_ref, expr_ref, in_sem,
     factors, part_src, part_buf, cross, vec_buf, vecs, grads_q, grads_r, grads_g,
-    peaks, kq, kr, kqt, krt, t_buf, prof_src, prof_buf, prof,
+    peaks, kq, kr, kqt, krt, t_buf, mate_kern, mate_expr, u_buf, scaled,
+    prof_src, prof_buf, prof,
     part_send, part_recv, vec_send, vec_recv, cross_send, cross_recv,
     fac_send, fac_recv, rank_send, rank_recv, vr_send, vr_recv,
-    peak_send, peak_recv, t_send, t_recv, prof_send, prof_recv, gat_send, gat_recv,
+    peak_send, peak_recv, t_send, t_recv, mate_send, mate_recv,
+    prof_send, prof_recv, gat_send, gat_recv, fwd_send, fwd_recv,
 ):
     me = lax.axis_index("cells")
     k = lax.axis_index("rank")
     near = k + 1 - 2 * lax.rem(k, 2)
     far = lax.rem(k + 2, 4)
     across = 3 - k
+    group, half = me // 2, lax.rem(me, 2)
+    groups = n // 2
+    mate = me + 1 - 2 * half
+
+    def each(first, last, body):
+        if last - first <= 8:
+            for i in range(first, last):
+                body(i)
+        else:
+            def one(i, carry):
+                body(i)
+                return carry
+            lax.fori_loop(first, last, one, 0)
 
     def peers(body):
-        if n <= 8:
-            for offset in range(1, n):
-                body(lax.rem(me + offset, n))
-        else:
-            def one(offset, carry):
-                body(lax.rem(me + offset, n))
-                return carry
-            lax.fori_loop(1, n, one, 0)
-
-    def only(limit, index, body):
-        if limit >= n:
+        each(1, n, lambda offset: body(lax.rem(me + offset, n)))
+
+    def lines(body):
+        each(1, groups, lambda offset: body(lax.rem(group + offset, groups)))
+
+    def only(limit, index, body, count=n):
+        if limit >= count:
             body()
         else:
             pl.when(index < limit)(body)
@@ -105,18 +119,36 @@
             device_id=(me, other), device_id_type=MESH,
         )
 
+    loads = [
+        pltpu.make_async_copy(src, dst, in_sem.at[i])
+        for i, (src, dst) in enumerate(
+            (
+                (q_hbm, q_ref), (x_hbm, x_ref), (r_hbm, r_ref), (y_hbm, y_ref),
+                (g_hbm, g_ref), (a_hbm, a_ref), (b_hbm, b_ref), (expr_hbm, expr_ref),
+            )
+        )
+    ]
+    for load in loads:
+        load.start()
     barrier = pltpu.get_barrier_semaphore()
     peers(lambda j: pl.semaphore_signal(barrier, inc=1, device_id=(j, k), device_id_type=MESH))
     for other in (near, far, across):
         pl.semaphore_signal(barrier, inc=1, device_id=(me, other), device_id_type=MESH)
 
-    x, y = x_ref[...], y_ref[...]
-    q, r = q_ref[...], r_ref[...]
-    q_round, r_round = q.astype(BF16), r.astype(BF16)
+    depth = part_src.shape[2]
+    loads[0].wait()
+    q = q_ref[...]
+    q_round = q.astype(BF16)
     factors[k, 0] = q_round
+    loads[1].wait()
+    x = x_ref[...]
+    part_src[:, 0] = contract_rows(x, q_round).astype(BF16).reshape(owners, depth, LANES)
+    loads[2].wait()
+    r = r_ref[...]
+    r_round = r.astype(BF16)
     factors[k, 1] = r_round
-    depth = part_src.shape[2]
-    part_src[:, 0] = contract_rows(x, q_round).astype(BF16).reshape(owners, depth, LANES)
+    loads[3].wait()
+    y = y_ref[...]
     part_src[:, 1] = contract_rows(y, r_round).astype(BF16).reshape(owners, depth, LANES)
     norms_one = jnp.sum(jnp.square(x.astype(F32)), axis=1, keepdims=True)
     norms_two = jnp.sum(jnp.square(y.astype(F32)), axis=1, keepdims=True)
@@ -130,6 +162,8 @@
         ],
         axis=0,
     )
+    for load in loads[4:]:
+        load.wait()
     pl.semaphore_wait(barrier, n - 1 + 3)
 
     def part_copy(j, slot):
@@ -167,7 +201,20 @@
     def cross_copy(j, slot):
         return to_peer(cross.at[k, slot], cross.at[k, slot], cross_send.at[j], cross_recv.at[slot], j)
 
-    only(owners, me, lambda: peers(lambda j: cross_copy(j, me).start()))
+    def rank_copy(slot, i, other, j):
+        return to_rank(
+            cross.at[slot, j], cross.at[slot, j], rank_send.at[i, j], rank_recv.at[i, j], other
+        )
+
+    def pass_on(j):
+        rank_copy(k, 1, far, j).start()
+        rank_copy(k, 0, near, j).start()
+
+    def send_cross():
+        peers(lambda j: cross_copy(j, me).start())
+        pass_on(me)
+
+    only(owners, me, send_cross)
 
     peers(lambda j: vec_copy(j, j).wait_recv())
     vec = vec_buf[0]
@@ -181,16 +228,22 @@
 
     for i, other in enumerate((near, far, across)):
         vecs_copy(k, i, other).start()
+
+    def arrived(j):
+        cross_copy(j, j).wait_recv()
+        pass_on(j)
+
+    peers(lambda j: only(owners, j, lambda: arrived(j)))
     factor_copy(far, 1, far).wait_recv()
     factor_copy(far, 2, near).start()
 
-    peers(lambda j: only(owners, j, lambda: cross_copy(j, j).wait_recv()))
-
-    def rank_copy(slot, i, other):
-        return to_rank(cross.at[slot], cross.at[slot], rank_send.at[i], rank_recv.at[i], other)
-
-    rank_copy(k, 1, far).start()
-    rank_copy(k, 0, near).start()
+    def mate_copy(i, src, dst):
+        return to_peer(src, dst, mate_send.at[i], mate_recv.at[i], mate)
+
+    expr_copy = mate_copy(0, expr_ref, mate_expr)
+    kern_copy = mate_copy(1, krt.at[1 - half], mate_kern)
+    u_copy = mate_copy(2, u_buf.at[0], u_buf.at[1])
+    expr_copy.start()
 
     def gradients(kk):
         info = vecs[kk]
@@ -214,14 +267,18 @@
 
     peak = gradients(k)
     vecs_copy(near, 0, near).wait_recv()
-    rank_copy(near, 0, near).wait_recv()
+    each(0, owners, lambda j: rank_copy(near, 0, near, j).wait_recv())
     peak = jnp.maximum(peak, gradients(near))
-    rank_copy(far, 1, far).wait_recv()
-    rank_copy(far, 2, near).start()
+
+    def across_x(j):
+        rank_copy(far, 1, far, j).wait_recv()
+        rank_copy(far, 2, near, j).start()
+
+    each(0, owners, across_x)
     vecs_copy(far, 1, far).wait_recv()
     peak = jnp.maximum(peak, gradients(far))
     vecs_copy(across, 2, across).wait_recv()
-    rank_copy(across, 2, near).wait_recv()
+    each(0, owners, lambda j: rank_copy(across, 2, near, j).wait_recv())
     peak = jnp.maximum(peak, gradients(across))
     peaks[me] = jnp.broadcast_to(peak, (8, LANES))
 
@@ -246,8 +303,10 @@
         kq[:, columns] = kern_q.astype(BF16)
         kr[:, columns] = kern_r.astype(BF16)
         kqt[columns, :] = jnp.transpose(kern_q).astype(BF16)
-        krt[columns, :] = jnp.transpose(kern_r).astype(BF16)
+        rows = slice(kk % 2 * LANES, (kk % 2 + 1) * LANES)
+        krt[kk // 2, rows, :] = jnp.transpose(kern_r).astype(BF16)
         log_g.append(jnp.log(vecs[kk][4:5]) - eta * grads_g[kk][0:1])
+    kern_copy.start()
     log_kern_g = jnp.concatenate(log_g + log_g, axis=0)
 
     def t_copy(parity, j, slot):
@@ -256,15 +315,21 @@
             t_send.at[parity, j], t_recv.at[parity, slot], j,
         )
 
-    def one_pass(step, carry):
-        v, _, _, _, _ = carry
-        parity = lax.rem(step, 2)
+    def whole_krt():
+        return krt[...].reshape(ranks * LANES, krt.shape[2])
+
+    def marginals(v):
+        s_r = row_product(wide(v, ranks, ranks), whole_krt())
+        u_r = jnp.exp(POWER * (log_b - jnp.log(s_r)))
         s_q = row_product(wide(v, 0, ranks), kqt[...])
-        s_r = row_product(wide(v, ranks, ranks), krt[...])
         u_q = jnp.exp(POWER * (log_a - jnp.log(s_q)))
-        u_r = jnp.exp(POWER * (log_b - jnp.log(s_r)))
+        return u_q, u_r
+
+    def send_t(parity, u_q, u_r):
         t_buf[parity, me] = tall(row_product(u_q, kq[...]), row_product(u_r, kr[...]))
         peers(lambda j: t_copy(parity, j, me).start())
+
+    def new_weights(parity, v):
         peers(lambda j: t_copy(parity, j, j).wait_recv())
         t = t_buf[parity, 0]
         for j in range(1, n):
@@ -273,68 +338,138 @@
         logs = jnp.log(v * t)
         other = jnp.concatenate([logs[ranks:], logs[:ranks]], axis=0)
         weights = jnp.exp((log_kern_g + logs + other) / 3.0)
-        return weights / t, weights, t, u_q, u_r
-
-    ones = jnp.ones((2 * ranks, LANES), F32)
-    row = jnp.ones((1, x.shape[0]), F32)
-    v, weights, t, u_q, u_r = lax.fori_loop(
-        0, PASSES, one_pass, (ones, ones, ones, row, row)
-    )
+        return weights / t, weights, t
+
+    def one_pass(step, v):
+        parity = lax.rem(step, 2)
+        send_t(parity, *marginals(v))
+        return new_weights(parity, v)[0]
+
+    v = lax.fori_loop(0, PASSES - 1, one_pass, jnp.ones((2 * ranks, LANES), F32))
+    u_q, u_r = marginals(v)
+    u_buf[0] = u_r
+    u_copy.start()
+    send_t((PASSES - 1) % 2, u_q, u_r)
 
     share = prof_src.shape[1]
-    left = (krt[...].astype(F32) * u_r).astype(BF16)
-    prof_src[...] = dot(left, expr_ref[...]).astype(BF16).reshape(prof_src.shape)
-
-    def prof_copy(j, slot):
-        return to_peer(prof_src.at[lax.rem(j, tiles)], prof_buf.at[slot], prof_send.at[j], prof_recv.at[slot], j)
-
-    peers(lambda j: only(tiles, j, lambda: prof_copy(j, me).start()))
+
+    def prof_copy(line, slot):
+        return to_peer(
+            prof_src.at[lax.rem(line, tiles)], prof_buf.at[slot],
+            prof_send.at[line], prof_recv.at[slot], 2 * line + half,
+        )
+
+    left = (krt[half].astype(F32) * u_r).astype(BF16)
+    total = dot(left, expr_ref[...])
+    expr_copy.wait_recv()
+    kern_copy.wait_recv()
+    u_copy.wait_recv()
+    left = (mate_kern[...].astype(F32) * u_buf[1]).astype(BF16)
+    total = total + dot(left, mate_expr[...])
+    prof_src[...] = total.astype(BF16).reshape(prof_src.shape)
+    lines(lambda line: only(tiles, line, lambda: prof_copy(line, group).start(), groups))
 
     def own_prof():
-        prof_buf[me] = prof_src[me]
-
-    only(tiles, me, own_prof)
-
+        prof_buf[group] = prof_src[group]
+
+    only(tiles, group, own_prof, groups)
+
+    v, weights, t = new_weights((PASSES - 1) % 2, v)
     w_out[...] = pick_row(weights, k) / cells_total
     own_q = q_ref[...] * jnp.exp(-eta * grads_q[k])
     own_r = r_ref[...] * jnp.exp(-eta * grads_r[k])
     q_out[...] = as_column(u_q) * own_q * pick_row(v, k)
     r_out[...] = as_column(u_r) * own_r * pick_row(v, k + ranks)
+    stores = [
+        pltpu.make_async_copy(src, dst, out_sem.at[i])
+        for i, (src, dst) in enumerate(
+            (
+                (q_out, q_hbm_out), (r_out, r_hbm_out),
+                (w_out, w_hbm_out), (pred_out, pred_hbm_out),
+            )
+        )
+    ]
+    for store in stores[:3]:
+        store.start()
     inverse = as_column(1.0 / row_product(wide(v, 0, ranks), kqt[...]))
-    scaled = (kq[...].astype(F32) * wide(v[ranks:] / t[:ranks], 0, ranks)).astype(BF16)
-
-    def gather_copy(j, slot):
-        return to_peer(prof.at[slot], prof.at[slot], gat_send.at[j], gat_recv.at[slot], j)
+    ratio = wide(v[ranks:] / t[:ranks], 0, ranks)
+    width = scaled.shape[2]
+    for i in range(2):
+        columns = slice(i * width, (i + 1) * width)
+        scaled[i] = (kq[:, columns].astype(F32) * ratio[:, columns]).astype(BF16)
+
+    def gather_copy(line, slot):
+        return to_peer(
+            prof.at[half, slot], prof.at[half, slot],
+            gat_send.at[line], gat_recv.at[slot], 2 * line + half,
+        )
+
+    def forward_copy(side, slot):
+        return to_peer(
+            prof.at[side, slot], prof.at[side, slot], fwd_send.at[slot], fwd_recv.at[slot], mate
+        )
 
     def reduce_prof():
-        peers(lambda j: prof_copy(j, j).wait_recv())
+        lines(lambda line: prof_copy(line, line).wait_recv())
         total = prof_buf[0].astype(F32)
-        for j in range(1, n):
-            total = total + prof_buf[j].astype(F32)
-        prof[me] = total.astype(BF16)
-        peers(lambda j: gather_copy(j, me).start())
-
-    only(tiles, me, reduce_prof)
-    peers(lambda j: only(tiles, j, lambda: gather_copy(j, j).wait_recv()))
-    mixed = dot(scaled, prof[...].reshape(tiles * share, prof.shape[2]))
+        for line in range(1, groups):
+            total = total + prof_buf[line].astype(F32)
+        prof[half, group] = total.astype(BF16)
+        lines(lambda line: gather_copy(line, group).start())
+        forward_copy(half, group).start()
+
+    only(tiles, group, reduce_prof, groups)
+
+    def gathered(line):
+        gather_copy(line, line).wait_recv()
+        forward_copy(half, line).start()
+
+    lines(lambda line: only(tiles, line, lambda: gathered(line), groups))
+    flat = (tiles * share, prof.shape[3])
+    mixed = dot(scaled[half], prof[half].reshape(flat))
+    each(0, tiles, lambda line: forward_copy(1 - half, line).wait_recv())
+    mixed = mixed + dot(scaled[1 - half], prof[1 - half].reshape(flat))
     for i in range(mixed.shape[1] // LANES):
         columns = slice(i * LANES, (i + 1) * LANES)
         pred_out[:, columns] = (mixed[:, columns] * inverse).astype(BF16)
+
+    stores[3].start()
 
     def sends(j):
         only(owners, j, lambda: part_copy(j, j).wait_send())
         vec_copy(j, j).wait_send()
         only(owners, me, lambda: cross_copy(j, me).wait_send())
         peak_copy(j, j).wait_send()
-        only(tiles, j, lambda: prof_copy(j, j).wait_send())
-        only(tiles, me, lambda: gather_copy(j, me).wait_send())
 
     peers(sends)
+
+    def line_sends(line):
+        only(tiles, line, lambda: prof_copy(line, line).wait_send(), groups)
+        only(tiles, group, lambda: gather_copy(line, group).wait_send(), groups)
+
+    lines(line_sends)
+    each(0, tiles, lambda line: forward_copy(half, line).wait_send())
+    for copy in (expr_copy, kern_copy, u_copy):
+        copy.wait_send()
     for i, (slot, other) in enumerate(((k, near), (k, far), (far, near))):
         factor_copy(slot, i, other).wait_send()
-        rank_copy(slot, i, other).wait_send()
+        each(0, owners, lambda j: rank_copy(slot, i, other, j).wait_send())
     for i, other in enumerate((near, far, across)):
         vecs_copy(k, i, other).wait_send()
+    for store in stores:
+        store.wait()
+
+
+def write_out(*refs):
+    count = len(refs) // 2
+    sem = refs[-1]
+    copies = [
+        pltpu.make_async_copy(refs[i], refs[count + i], sem.at[i]) for i in range(count)
+    ]
+    for copy in copies:
+        copy.start()
+    for copy in copies:
+        copy.wait()
 
 
 def shards(n, ranks, x_emb, y_emb, q_factor, r_factor, g_weights, a_mass, b_mass, expr):
@@ -342,22 +477,40 @@
     genes = expr.shape[1]
     rank_all = ranks * LANES
     owners = min(n, dim // 16)
-    tiles = min(n, rank_all // 16)
-    vmem = pl.BlockSpec(memory_space=pltpu.VMEM)
+    groups = n // 2
+    tiles = min(groups, rank_all // 2 // 16)
+    hbm = pl.BlockSpec(memory_space=pltpu.HBM)
     dma = pltpu.SemaphoreType.DMA
     pair = [dma((n,)), dma((n,))]
     three = [dma((3,)), dma((3,))]
-    q_new, r_new, rank_share, predicted = pl.pallas_call(
+    lined = [dma((groups,)), dma((groups,))]
+    block = (rank_all // 2 // tiles, genes)
+    shapes = (
+        jax.ShapeDtypeStruct(q_factor.shape, F32),
+        jax.ShapeDtypeStruct(r_factor.shape, F32),
+        jax.ShapeDtypeStruct((1, LANES), F32),
+        jax.ShapeDtypeStruct((rows, genes), BF16),
+    )
+    results = pl.pallas_call(
         functools.partial(kernel, n, ranks, owners, tiles, float(rows * n)),
-        out_shape=(
-            jax.ShapeDtypeStruct(q_factor.shape, F32),
-            jax.ShapeDtypeStruct(r_factor.shape, F32),
-            jax.ShapeDtypeStruct((1, LANES), F32),
-            jax.ShapeDtypeStruct((rows, genes), BF16),
-        ),
-        in_specs=[vmem] * 8,
-        out_specs=(vmem,) * 4,
+        out_shape=shapes,
+        in_specs=[hbm] * 8,
+        out_specs=(hbm,) * 4,
         scratch_shapes=[
+            pltpu.VMEM(q_factor.shape, F32),
+            pltpu.VMEM(r_factor.shape, F32),
+            pltpu.VMEM((1, LANES), F32),
+            pltpu.VMEM((rows, genes), BF16),
+            dma((4,)),
+            pltpu.VMEM(x_emb.shape, BF16),
+            pltpu.VMEM(y_emb.shape, BF16),
+            pltpu.VMEM(q_factor.shape, F32),
+            pltpu.VMEM(r_factor.shape, F32),
+            pltpu.VMEM((1, LANES), F32),
+            pltpu.VMEM((1, rows), F32),
+            pltpu.VMEM((1, rows), F32),
+            pltpu.VMEM(expr.shape, BF16),
+            dma((8,)),
             pltpu.VMEM((ranks, 2, rows, LANES), BF16),
             pltpu.VMEM((owners, 2, dim // owners, LANES), BF16),
             pltpu.VMEM((n, 2, dim // owners, LANES), BF16),
@@ -371,17 +524,23 @@
             pltpu.VMEM((rows, rank_all), BF16),
             pltpu.VMEM((rows, rank_all), BF16),
             pltpu.VMEM((rank_all, rows), BF16),
-            pltpu.VMEM((rank_all, rows), BF16),
+            pltpu.VMEM((2, rank_all // 2, rows), BF16),
             pltpu.VMEM((2, n, 8, LANES), F32),
-            pltpu.VMEM((tiles, rank_all // tiles, genes), BF16),
-            pltpu.VMEM((n, rank_all // tiles, genes), BF16),
-            pltpu.VMEM((tiles, rank_all // tiles, genes), BF16),
+            pltpu.VMEM((rank_all // 2, rows), BF16),
+            pltpu.VMEM(expr.shape, BF16),
+            pltpu.VMEM((2, 1, rows), F32),
+            pltpu.VMEM((2, rows, rank_all // 2), BF16),
+            pltpu.VMEM((tiles,) + block, BF16),
+            pltpu.VMEM((groups,) + block, BF16),
+            pltpu.VMEM((2, tiles) + block, BF16),
         ]
-        + pair + pair + pair + three + three + three + pair
+        + pair + pair + pair + three
+        + [dma((3, owners)), dma((3, owners))]
+        + three + pair
         + [dma((2, n)), dma((2, n))]
-        + pair + pair,
+        + three + lined + lined + lined,
         compiler_params=pltpu.CompilerParams(
-            collective_id=0, has_side_effects=True, vmem_limit_bytes=48 * 1024 * 1024
+            collective_id=0, has_side_effects=True, vmem_limit_bytes=VMEM_LIMIT
         ),
         cost_estimate=pl.CostEstimate(
             flops=2 * rows * (2 * dim * LANES + 2 * dim * rank_all + 2 * rank_all * genes),
@@ -393,6 +552,15 @@
         x_emb, y_emb, q_factor, r_factor, g_weights.reshape(1, LANES),
         a_mass.reshape(1, rows), b_mass.reshape(1, rows), expr,
     )
+    q_new, r_new, rank_share, predicted = pl.pallas_call(
+        write_out,
+        out_shape=shapes,
+        in_specs=[hbm] * 4,
+        out_specs=(hbm,) * 4,
+        scratch_shapes=[dma((4,))],
+        compiler_params=pltpu.CompilerParams(vmem_limit_bytes=VMEM_LIMIT),
+        name="write_out",
+    )(*results)
     return q_new, r_new, rank_share.reshape(LANES), predicted
 
 

time: 100 us -> 124 us (1.24)
  Pallas kernels: 91.3 us -> 123 us
  local copies, waits for them, and re-layouts: 8.23 us -> 0 us
    pallas_call x0 -> x1, Pallas kernels: none -> 32.9 us  [shards(): pl.pallas_call(write_out, out_shape=shapes, in_specs=[hbm] * 4, out_specs...]
    unnamed x20 -> x0, local copies, waits for them, and re-layouts: 8.23 us -> none
where the time goes in v2:
time: 124 us
  Pallas kernels  123 us (99%)
    pallas_call x1, Pallas kernels, shards(): pl.pallas_call(functools.partial(kernel, n, ranks, owners, tiles, float(r...  90.1 us
    pallas_call x1, Pallas kernels, shards(): pl.pallas_call(write_out, out_shape=shapes, in_specs=[hbm] * 4, out_specs...  32.9 us

profile of v2, /device:TPU:0, one launch (start us, length us, event | category | flops | bytes accessed | tf_op | source)
XLA Modules:
  0.0 123.7 jit_solution(11113528534700160917)
XLA Ops:
  0.6 90.1 %transport_step.1 = (f32[512,128]{1,0:T(8,128)}, f32[512,128]{1,0:T(8,128)}, f32[1,128]{1,0:T(1,128)}, bf16[512,512]{1,0:T(8,128)(2,1)}) custom-call(bf16[512,256]{1,0:T(8,128)(2,1)} %x_hbm.1, bf16[512,256]{1,0:T(8,128)(2,1)} %y_hbm.1, f32[512,128]{1,0:T(8,128)} %q_hbm.1, f32[512,128]{1,0:T(8,128)} %r_hbm.1, f32[1,128]{1,0:T(1,128)} %bitcast.6, ...), custom_call_target="tpu_custom_call" | custom-call | flops 872415232 | bytes 4194304 | tf_op jit(solution)/shard_map/transport_step/pallas_call | solution.py:494
  90.8 32.9 %write_out.1 = (f32[512,128]{1,0:T(8,128)}, f32[512,128]{1,0:T(8,128)}, f32[1,128]{1,0:T(1,128)}, bf16[512,512]{1,0:T(8,128)(2,1)}) custom-call(f32[512,128]{1,0:T(8,128)} %get-tuple-element.12.refs_0_, f32[512,128]{1,0:T(8,128)} %get-tuple-element.13.refs_1_, f32[1,128]{1,0:T(1,128)} %get-tuple-element.14.refs_2_, bf16[512,512]{1,0:T(8,128)(2,1)} %get-tuple-element.15.refs_3_), custom_call_target="tpu_custom_call" | custom-call | tf_op jit(solution)/shard_map/write_out/pallas_call | solution.py:555

commit v3 on v2

--- a/solution.py
+++ b/solution.py
@@ -8,6 +8,7 @@
 from jax.sharding import PartitionSpec as P
 
 PASSES = 10
+PIECES = 8
 SCALE = 0.0625
 GAMMA = 10.0
 POWER = 0.8
@@ -95,11 +96,25 @@
                 return carry
             lax.fori_loop(first, last, one, 0)
 
-    def peers(body):
-        each(1, n, lambda offset: body(lax.rem(me + offset, n)))
-
-    def lines(body):
-        each(1, groups, lambda offset: body(lax.rem(group + offset, groups)))
+    def others(index, count):
+        if count > 8 or count & (count - 1):
+            return lambda body: each(1, count, lambda offset: body(lax.rem(index + offset, count)))
+        found = []
+        for offset in range(count - 1, 0, -1):
+            other = index
+            for bit in (1, 2, 4):
+                if offset & bit:
+                    other = other + bit - 2 * bit * lax.rem(index // bit, 2)
+            found.append(other)
+
+        def over(body):
+            for other in found:
+                body(other)
+
+        return over
+
+    peers = others(me, n)
+    lines = others(group, groups)
 
     def only(limit, index, body, count=n):
         if limit >= count:
@@ -150,6 +165,24 @@
     loads[3].wait()
     y = y_ref[...]
     part_src[:, 1] = contract_rows(y, r_round).astype(BF16).reshape(owners, depth, LANES)
+    for load in loads[4:]:
+        load.wait()
+    pl.semaphore_wait(barrier, n - 1 + 3)
+
+    def part_copy(j, slot):
+        return to_peer(part_src.at[lax.rem(j, owners)], part_buf.at[slot], part_send.at[j], part_recv.at[slot], j)
+
+    def vec_copy(j, slot):
+        return to_peer(vec_buf.at[me], vec_buf.at[slot], vec_send.at[j], vec_recv.at[slot], j)
+
+    peers(lambda j: only(owners, j, lambda: part_copy(j, me).start()))
+
+    def factor_copy(slot, i, other):
+        return to_rank(factors.at[slot], factors.at[slot], fac_send.at[i], fac_recv.at[i], other)
+
+    factor_copy(k, 0, near).start()
+    factor_copy(k, 1, far).start()
+
     norms_one = jnp.sum(jnp.square(x.astype(F32)), axis=1, keepdims=True)
     norms_two = jnp.sum(jnp.square(y.astype(F32)), axis=1, keepdims=True)
     vec_buf[me] = jnp.concatenate(
@@ -162,27 +195,7 @@
         ],
         axis=0,
     )
-    for load in loads[4:]:
-        load.wait()
-    pl.semaphore_wait(barrier, n - 1 + 3)
-
-    def part_copy(j, slot):
-        return to_peer(part_src.at[lax.rem(j, owners)], part_buf.at[slot], part_send.at[j], part_recv.at[slot], j)
-
-    def vec_copy(j, slot):
-        return to_peer(vec_buf.at[me], vec_buf.at[slot], vec_send.at[j], vec_recv.at[slot], j)
-
-    def send_parts(j):
-        only(owners, j, lambda: part_copy(j, me).start())
-        vec_copy(j, me).start()
-
-    peers(send_parts)
-
-    def factor_copy(slot, i, other):
-        return to_rank(factors.at[slot], factors.at[slot], fac_send.at[i], fac_recv.at[i], other)
-
-    factor_copy(k, 0, near).start()
-    factor_copy(k, 1, far).start()
+    peers(lambda j: vec_copy(j, me).start())
 
     def own_part():
         part_buf[me] = part_src[me]
@@ -237,13 +250,22 @@
     factor_copy(far, 1, far).wait_recv()
     factor_copy(far, 2, near).start()
 
-    def mate_copy(i, src, dst):
-        return to_peer(src, dst, mate_send.at[i], mate_recv.at[i], mate)
-
-    expr_copy = mate_copy(0, expr_ref, mate_expr)
-    kern_copy = mate_copy(1, krt.at[1 - half], mate_kern)
-    u_copy = mate_copy(2, u_buf.at[0], u_buf.at[1])
-    expr_copy.start()
+    def expr_copy(piece):
+        size = expr_ref.shape[0] // PIECES
+        rows = pl.ds(pl.multiple_of(piece * size, size), size)
+        return to_peer(
+            expr_ref.at[rows], mate_expr.at[rows], mate_send.at[0, piece], mate_recv.at[0, piece], mate
+        )
+
+    def kern_copy(piece):
+        size = mate_kern.shape[0] // PIECES
+        rows = pl.ds(pl.multiple_of(piece * size, size), size)
+        return to_peer(
+            krt.at[1 - half, rows], mate_kern.at[rows],
+            mate_send.at[1, piece], mate_recv.at[1, piece], mate,
+        )
+
+    u_copy = to_peer(u_buf.at[0], u_buf.at[1], mate_send.at[2, 0], mate_recv.at[2, 0], mate)
 
     def gradients(kk):
         info = vecs[kk]
@@ -300,13 +322,13 @@
         columns = slice(kk * LANES, (kk + 1) * LANES)
         kern_q = factors[kk, 0].astype(F32) * jnp.exp(-eta * grads_q[kk])
         kern_r = factors[kk, 1].astype(F32) * jnp.exp(-eta * grads_r[kk])
-        kq[:, columns] = kern_q.astype(BF16)
-        kr[:, columns] = kern_r.astype(BF16)
-        kqt[columns, :] = jnp.transpose(kern_q).astype(BF16)
+        kern_q, kern_r = kern_q.astype(BF16), kern_r.astype(BF16)
+        kq[:, columns] = kern_q
+        kr[:, columns] = kern_r
+        kqt[columns, :] = jnp.transpose(kern_q)
         rows = slice(kk % 2 * LANES, (kk % 2 + 1) * LANES)
-        krt[kk // 2, rows, :] = jnp.transpose(kern_r).astype(BF16)
+        krt[kk // 2, rows, :] = jnp.transpose(kern_r)
         log_g.append(jnp.log(vecs[kk][4:5]) - eta * grads_g[kk][0:1])
-    kern_copy.start()
     log_kern_g = jnp.concatenate(log_g + log_g, axis=0)
 
     def t_copy(parity, j, slot):
@@ -343,6 +365,12 @@
     def one_pass(step, v):
         parity = lax.rem(step, 2)
         send_t(parity, *marginals(v))
+
+        @pl.when(step < PIECES)
+        def send_piece():
+            expr_copy(step).start()
+            kern_copy(step).start()
+
         return new_weights(parity, v)[0]
 
     v = lax.fori_loop(0, PASSES - 1, one_pass, jnp.ones((2 * ranks, LANES), F32))
@@ -361,8 +389,9 @@
 
     left = (krt[half].astype(F32) * u_r).astype(BF16)
     total = dot(left, expr_ref[...])
-    expr_copy.wait_recv()
-    kern_copy.wait_recv()
+    for piece in range(PIECES):
+        expr_copy(piece).wait_recv()
+        kern_copy(piece).wait_recv()
     u_copy.wait_recv()
     left = (mate_kern[...].astype(F32) * u_buf[1]).astype(BF16)
     total = total + dot(left, mate_expr[...])
@@ -449,8 +478,10 @@
 
     lines(line_sends)
     each(0, tiles, lambda line: forward_copy(half, line).wait_send())
-    for copy in (expr_copy, kern_copy, u_copy):
-        copy.wait_send()
+    u_copy.wait_send()
+    for piece in range(PIECES):
+        expr_copy(piece).wait_send()
+        kern_copy(piece).wait_send()
     for i, (slot, other) in enumerate(((k, near), (k, far), (far, near))):
         factor_copy(slot, i, other).wait_send()
         each(0, owners, lambda j: rank_copy(slot, i, other, j).wait_send())
@@ -460,16 +491,22 @@
         store.wait()
 
 
-def write_out(*refs):
-    count = len(refs) // 2
-    sem = refs[-1]
-    copies = [
-        pltpu.make_async_copy(refs[i], refs[count + i], sem.at[i]) for i in range(count)
+def write_out(count, *refs):
+    sources, results, held = (refs[i * count : (i + 1) * count] for i in range(3))
+    load_sem, store_sem = refs[3 * count :]
+    loads = [
+        pltpu.make_async_copy(sources[i], held[i], load_sem.at[i]) for i in range(count)
     ]
-    for copy in copies:
-        copy.start()
-    for copy in copies:
-        copy.wait()
+    stores = [
+        pltpu.make_async_copy(held[i], results[i], store_sem.at[i]) for i in range(count)
+    ]
+    for load in loads:
+        load.start()
+    for load, store in zip(loads, stores):
+        load.wait()
+        store.start()
+    for store in stores:
+        store.wait()
 
 
 def shards(n, ranks, x_emb, y_emb, q_factor, r_factor, g_weights, a_mass, b_mass, expr):
@@ -538,7 +575,8 @@
         + [dma((3, owners)), dma((3, owners))]
         + three + pair
         + [dma((2, n)), dma((2, n))]
-        + three + lined + lined + lined,
+        + [dma((3, PIECES)), dma((3, PIECES))]
+        + lined + lined + lined,
         compiler_params=pltpu.CompilerParams(
             collective_id=0, has_side_effects=True, vmem_limit_bytes=VMEM_LIMIT
         ),
@@ -553,11 +591,12 @@
         a_mass.reshape(1, rows), b_mass.reshape(1, rows), expr,
     )
     q_new, r_new, rank_share, predicted = pl.pallas_call(
-        write_out,
+        functools.partial(write_out, len(shapes)),
         out_shape=shapes,
         in_specs=[hbm] * 4,
         out_specs=(hbm,) * 4,
-        scratch_shapes=[dma((4,))],
+        scratch_shapes=[pltpu.VMEM(shape.shape, shape.dtype) for shape in shapes]
+        + [dma((len(shapes),)), dma((len(shapes),))],
         compiler_params=pltpu.CompilerParams(vmem_limit_bytes=VMEM_LIMIT),
         name="write_out",
     )(*results)

time: 124 us -> 89.8 us (0.72)
  Pallas kernels: 123 us -> 89 us
    pallas_call x1, Pallas kernels: 32.9 us -> 2.07 us  [shards(): pl.pallas_call(functools.partial(write_out, len(shapes)), out_shape=shape...]
    pallas_call x1, Pallas kernels: 90.1 us -> 86.9 us  [shards(): pl.pallas_call(functools.partial(kernel, n, ranks, owners, tiles, float(r...]
where the time goes in v3:
time: 89.8 us; the launch traced here: 89.6 us
  Pallas kernels  89 us (99%)
    pallas_call x1, Pallas kernels, shards(): pl.pallas_call(functools.partial(kernel, n, ranks, owners, tiles, float(r...  86.9 us
    pallas_call x1, Pallas kernels, shards(): pl.pallas_call(functools.partial(write_out, len(shapes)), out_shape=shape...  2.07 us

profile of v3, /device:TPU:0, one launch (start us, length us, event | category | flops | bytes accessed | tf_op | source)
XLA Modules:
  0.0 89.6 jit_solution(18078957257233912186)
XLA Ops:
  0.6 86.9 %transport_step.1 = (f32[512,128]{1,0:T(8,128)}, f32[512,128]{1,0:T(8,128)}, f32[1,128]{1,0:T(1,128)}, bf16[512,512]{1,0:T(8,128)(2,1)}) custom-call(bf16[512,256]{1,0:T(8,128)(2,1)} %x_hbm.1, bf16[512,256]{1,0:T(8,128)(2,1)} %y_hbm.1, f32[512,128]{1,0:T(8,128)} %q_hbm.1, f32[512,128]{1,0:T(8,128)} %r_hbm.1, f32[1,128]{1,0:T(1,128)} %bitcast.6, ...), custom_call_target="tpu_custom_call" | custom-call | flops 872415232 | bytes 4194304 | tf_op jit(solution)/shard_map/transport_step/pallas_call | solution.py:531
  87.6 2.1 %write_out.1 = (f32[512,128]{1,0:T(8,128)}, f32[512,128]{1,0:T(8,128)}, f32[1,128]{1,0:T(1,128)}, bf16[512,512]{1,0:T(8,128)(2,1)}) custom-call(f32[512,128]{1,0:T(8,128)} %get-tuple-element.12.refs_0_, f32[512,128]{1,0:T(8,128)} %get-tuple-element.13.refs_1_, f32[1,128]{1,0:T(1,128)} %get-tuple-element.14.refs_2_, bf16[512,512]{1,0:T(8,128)(2,1)} %get-tuple-element.15.refs_3_), custom_call_target="tpu_custom_call" | custom-call | tf_op jit(solution)/shard_map/write_out/pallas_call | solution.py:593

commit v4 on v3

--- a/solution.py
+++ b/solution.py
@@ -9,6 +9,7 @@
 
 PASSES = 10
 PIECES = 8
+BLOCKS = 4
 SCALE = 0.0625
 GAMMA = 10.0
 POWER = 0.8
@@ -98,7 +99,9 @@
 
     def others(index, count):
         if count > 8 or count & (count - 1):
-            return lambda body: each(1, count, lambda offset: body(lax.rem(index + offset, count)))
+            return lambda body, reverse=False: each(
+                1, count, lambda offset: body(lax.rem(index + offset, count))
+            )
         found = []
         for offset in range(count - 1, 0, -1):
             other = index
@@ -107,8 +110,8 @@
                     other = other + bit - 2 * bit * lax.rem(index // bit, 2)
             found.append(other)
 
-        def over(body):
-            for other in found:
+        def over(body, reverse=False):
+            for other in found[::-1] if reverse else found:
                 body(other)
 
         return over
@@ -133,6 +136,10 @@
             src_ref=src, dst_ref=dst, send_sem=send, recv_sem=recv,
             device_id=(me, other), device_id_type=MESH,
         )
+
+    def all_copies(slots, send, recv):
+        most = slots.at[pl.ds(0, n - 1)]
+        return to_peer(most, most, send, recv, mate)
 
     loads = [
         pltpu.make_async_copy(src, dst, in_sem.at[i])
@@ -173,7 +180,7 @@
         return to_peer(part_src.at[lax.rem(j, owners)], part_buf.at[slot], part_send.at[j], part_recv.at[slot], j)
 
     def vec_copy(j, slot):
-        return to_peer(vec_buf.at[me], vec_buf.at[slot], vec_send.at[j], vec_recv.at[slot], j)
+        return to_peer(vec_buf.at[me], vec_buf.at[slot], vec_send.at[0], vec_recv.at[0], j)
 
     peers(lambda j: only(owners, j, lambda: part_copy(j, me).start()))
 
@@ -229,7 +236,7 @@
 
     only(owners, me, send_cross)
 
-    peers(lambda j: vec_copy(j, j).wait_recv())
+    all_copies(vec_buf, vec_send.at[0], vec_recv.at[0]).wait_recv()
     vec = vec_buf[0]
     for j in range(1, n):
         vec = vec + vec_buf[j]
@@ -246,7 +253,7 @@
         cross_copy(j, j).wait_recv()
         pass_on(j)
 
-    peers(lambda j: only(owners, j, lambda: arrived(j)))
+    peers(lambda j: only(owners, j, lambda: arrived(j)), reverse=True)
     factor_copy(far, 1, far).wait_recv()
     factor_copy(far, 2, near).start()
 
@@ -305,13 +312,13 @@
     peaks[me] = jnp.broadcast_to(peak, (8, LANES))
 
     def peak_copy(j, slot):
-        return to_peer(peaks.at[me], peaks.at[slot], peak_send.at[j], peak_recv.at[slot], j)
+        return to_peer(peaks.at[me], peaks.at[slot], peak_send.at[0], peak_recv.at[0], j)
 
     peers(lambda j: peak_copy(j, me).start())
     factor_copy(near, 0, near).wait_recv()
     factor_copy(across, 2, near).wait_recv()
     log_a, log_b = jnp.log(a_ref[...]), jnp.log(b_ref[...])
-    peers(lambda j: peak_copy(j, j).wait_recv())
+    all_copies(peaks, peak_send.at[0], peak_recv.at[0]).wait_recv()
     top = peaks[0]
     for j in range(1, n):
         top = jnp.maximum(top, peaks[j])
@@ -334,8 +341,11 @@
     def t_copy(parity, j, slot):
         return to_peer(
             t_buf.at[parity, me], t_buf.at[parity, slot],
-            t_send.at[parity, j], t_recv.at[parity, slot], j,
-        )
+            t_send.at[parity], t_recv.at[parity], j,
+        )
+
+    def t_all(parity):
+        return all_copies(t_buf.at[parity], t_send.at[parity], t_recv.at[parity])
 
     def whole_krt():
         return krt[...].reshape(ranks * LANES, krt.shape[2])
@@ -352,11 +362,11 @@
         peers(lambda j: t_copy(parity, j, me).start())
 
     def new_weights(parity, v):
-        peers(lambda j: t_copy(parity, j, j).wait_recv())
+        t_all(parity).wait_recv()
         t = t_buf[parity, 0]
         for j in range(1, n):
             t = t + t_buf[parity, j]
-        peers(lambda j: t_copy(parity, j, j).wait_send())
+        t_all(parity).wait_send()
         logs = jnp.log(v * t)
         other = jnp.concatenate([logs[ranks:], logs[:ranks]], axis=0)
         weights = jnp.exp((log_kern_g + logs + other) / 3.0)
@@ -404,17 +414,42 @@
     only(tiles, group, own_prof, groups)
 
     v, weights, t = new_weights((PASSES - 1) % 2, v)
+
+    def sends(j):
+        only(owners, j, lambda: part_copy(j, j).wait_send())
+        only(owners, me, lambda: cross_copy(j, me).wait_send())
+
+    peers(sends)
+    all_copies(vec_buf, vec_send.at[0], vec_recv.at[0]).wait_send()
+    all_copies(peaks, peak_send.at[0], peak_recv.at[0]).wait_send()
+    for i, (slot, other) in enumerate(((k, near), (k, far), (far, near))):
+        factor_copy(slot, i, other).wait_send()
+        each(0, owners, lambda j: rank_copy(slot, i, other, j).wait_send())
+    for i, other in enumerate((near, far, across)):
+        vecs_copy(k, i, other).wait_send()
+    u_copy.wait_send()
+    for piece in range(PIECES):
+        expr_copy(piece).wait_send()
+        kern_copy(piece).wait_send()
     w_out[...] = pick_row(weights, k) / cells_total
     own_q = q_ref[...] * jnp.exp(-eta * grads_q[k])
     own_r = r_ref[...] * jnp.exp(-eta * grads_r[k])
     q_out[...] = as_column(u_q) * own_q * pick_row(v, k)
     r_out[...] = as_column(u_r) * own_r * pick_row(v, k + ranks)
+    def block_rows(i):
+        size = pred_out.shape[0] // BLOCKS
+        return slice(i * size, (i + 1) * size)
+
     stores = [
         pltpu.make_async_copy(src, dst, out_sem.at[i])
         for i, (src, dst) in enumerate(
             (
                 (q_out, q_hbm_out), (r_out, r_hbm_out),
-                (w_out, w_hbm_out), (pred_out, pred_hbm_out),
+                (w_out, w_hbm_out),
+            )
+            + tuple(
+                (pred_out.at[block_rows(i)], pred_hbm_out.at[block_rows(i)])
+                for i in range(BLOCKS)
             )
         )
     ]
@@ -453,40 +488,23 @@
         gather_copy(line, line).wait_recv()
         forward_copy(half, line).start()
 
-    lines(lambda line: only(tiles, line, lambda: gathered(line), groups))
+    lines(lambda line: only(tiles, line, lambda: gathered(line), groups), reverse=True)
     flat = (tiles * share, prof.shape[3])
-    mixed = dot(scaled[half], prof[half].reshape(flat))
     each(0, tiles, lambda line: forward_copy(1 - half, line).wait_recv())
-    mixed = mixed + dot(scaled[1 - half], prof[1 - half].reshape(flat))
-    for i in range(mixed.shape[1] // LANES):
-        columns = slice(i * LANES, (i + 1) * LANES)
-        pred_out[:, columns] = (mixed[:, columns] * inverse).astype(BF16)
-
-    stores[3].start()
-
-    def sends(j):
-        only(owners, j, lambda: part_copy(j, j).wait_send())
-        vec_copy(j, j).wait_send()
-        only(owners, me, lambda: cross_copy(j, me).wait_send())
-        peak_copy(j, j).wait_send()
-
-    peers(sends)
-
-    def line_sends(line):
-        only(tiles, line, lambda: prof_copy(line, line).wait_send(), groups)
+    for i in range(BLOCKS):
+        rows = block_rows(i)
+        mixed = dot(scaled[half, rows], prof[half].reshape(flat))
+        mixed = mixed + dot(scaled[1 - half, rows], prof[1 - half].reshape(flat))
+        across_genes = jnp.concatenate([inverse[rows]] * (mixed.shape[1] // LANES), axis=1)
+        pred_out[rows] = (mixed * across_genes).astype(BF16)
+        stores[3 + i].start()
+
+    def last_sends(line):
         only(tiles, group, lambda: gather_copy(line, group).wait_send(), groups)
 
-    lines(line_sends)
+    lines(last_sends)
+    lines(lambda line: only(tiles, line, lambda: prof_copy(line, line).wait_send(), groups))
     each(0, tiles, lambda line: forward_copy(half, line).wait_send())
-    u_copy.wait_send()
-    for piece in range(PIECES):
-        expr_copy(piece).wait_send()
-        kern_copy(piece).wait_send()
-    for i, (slot, other) in enumerate(((k, near), (k, far), (far, near))):
-        factor_copy(slot, i, other).wait_send()
-        each(0, owners, lambda j: rank_copy(slot, i, other, j).wait_send())
-    for i, other in enumerate((near, far, across)):
-        vecs_copy(k, i, other).wait_send()
     for store in stores:
         store.wait()
 
@@ -494,12 +512,19 @@
 def write_out(count, *refs):
     sources, results, held = (refs[i * count : (i + 1) * count] for i in range(3))
     load_sem, store_sem = refs[3 * count :]
-    loads = [
-        pltpu.make_async_copy(sources[i], held[i], load_sem.at[i]) for i in range(count)
-    ]
-    stores = [
-        pltpu.make_async_copy(held[i], results[i], store_sem.at[i]) for i in range(count)
-    ]
+    loads, stores = [], []
+    for source, result, hold in zip(sources, results, held):
+        pieces = BLOCKS if source.shape[0] > BLOCKS else 1
+        size = source.shape[0] // pieces
+        for i in range(pieces):
+            rows = pl.ds(i * size, size)
+            sem = len(loads)
+            loads.append(
+                pltpu.make_async_copy(source.at[rows], hold.at[rows], load_sem.at[sem])
+            )
+            stores.append(
+                pltpu.make_async_copy(hold.at[rows], result.at[rows], store_sem.at[sem])
+            )
     for load in loads:
         load.start()
     for load, store in zip(loads, stores):
@@ -519,6 +544,7 @@
     hbm = pl.BlockSpec(memory_space=pltpu.HBM)
     dma = pltpu.SemaphoreType.DMA
     pair = [dma((n,)), dma((n,))]
+    single = [dma((1,)), dma((1,))]
     three = [dma((3,)), dma((3,))]
     lined = [dma((groups,)), dma((groups,))]
     block = (rank_all // 2 // tiles, genes)
@@ -538,7 +564,7 @@
             pltpu.VMEM(r_factor.shape, F32),
             pltpu.VMEM((1, LANES), F32),
             pltpu.VMEM((rows, genes), BF16),
-            dma((4,)),
+            dma((3 + BLOCKS,)),
             pltpu.VMEM(x_emb.shape, BF16),
             pltpu.VMEM(y_emb.shape, BF16),
             pltpu.VMEM(q_factor.shape, F32),
@@ -571,10 +597,10 @@
             pltpu.VMEM((groups,) + block, BF16),
             pltpu.VMEM((2, tiles) + block, BF16),
         ]
-        + pair + pair + pair + three
+        + pair + single + pair + three
         + [dma((3, owners)), dma((3, owners))]
-        + three + pair
-        + [dma((2, n)), dma((2, n))]
+        + three + single
+        + [dma((2,)), dma((2,))]
         + [dma((3, PIECES)), dma((3, PIECES))]
         + lined + lined + lined,
         compiler_params=pltpu.CompilerParams(
@@ -596,7 +622,7 @@
         in_specs=[hbm] * 4,
         out_specs=(hbm,) * 4,
         scratch_shapes=[pltpu.VMEM(shape.shape, shape.dtype) for shape in shapes]
-        + [dma((len(shapes),)), dma((len(shapes),))],
+        + [dma((len(shapes) * BLOCKS,)), dma((len(shapes) * BLOCKS,))],
         compiler_params=pltpu.CompilerParams(vmem_limit_bytes=VMEM_LIMIT),
         name="write_out",
     )(*results)

time: 89.8 us -> 88.1 us (0.981)
  Pallas kernels: 89 us -> 87.3 us
    pallas_call x1, Pallas kernels: 86.9 us -> 85.1 us  [shards(): pl.pallas_call(functools.partial(kernel, n, ranks, owners, tiles, float(r...]
where the time goes in v4:
time: 88.1 us; the launch traced here: 88 us
  Pallas kernels  87.3 us (99%)
    pallas_call x1, Pallas kernels, shards(): pl.pallas_call(functools.partial(kernel, n, ranks, owners, tiles, float(r...  85.1 us
    pallas_call x1, Pallas kernels, shards(): pl.pallas_call(functools.partial(write_out, len(shapes)), out_shape=shape...  2.24 us

profile of v4, /device:TPU:0, one launch (start us, length us, event | category | flops | bytes accessed | tf_op | source)
XLA Modules:
  0.0 88.0 jit_solution(17117470387305187188)
XLA Ops:
  0.6 85.1 %transport_step.1 = (f32[512,128]{1,0:T(8,128)}, f32[512,128]{1,0:T(8,128)}, f32[1,128]{1,0:T(1,128)}, bf16[512,512]{1,0:T(8,128)(2,1)}) custom-call(bf16[512,256]{1,0:T(8,128)(2,1)} %x_hbm.1, bf16[512,256]{1,0:T(8,128)(2,1)} %y_hbm.1, f32[512,128]{1,0:T(8,128)} %q_hbm.1, f32[512,128]{1,0:T(8,128)} %r_hbm.1, f32[1,128]{1,0:T(1,128)} %bitcast.6, ...), custom_call_target="tpu_custom_call" | custom-call | flops 872415232 | bytes 4194304 | tf_op jit(solution)/shard_map/transport_step/pallas_call | solution.py:557
  85.7 2.2 %write_out.1 = (f32[512,128]{1,0:T(8,128)}, f32[512,128]{1,0:T(8,128)}, f32[1,128]{1,0:T(1,128)}, bf16[512,512]{1,0:T(8,128)(2,1)}) custom-call(f32[512,128]{1,0:T(8,128)} %get-tuple-element.12.refs_0_, f32[512,128]{1,0:T(8,128)} %get-tuple-element.13.refs_1_, f32[1,128]{1,0:T(1,128)} %get-tuple-element.14.refs_2_, bf16[512,512]{1,0:T(8,128)(2,1)} %get-tuple-element.15.refs_3_), custom_call_target="tpu_custom_call" | custom-call | tf_op jit(solution)/shard_map/write_out/pallas_call | solution.py:619

commit v5 on v4

--- a/solution.py
+++ b/solution.py
@@ -10,6 +10,7 @@
 PASSES = 10
 PIECES = 8
 BLOCKS = 4
+HALVES = 2
 SCALE = 0.0625
 GAMMA = 10.0
 POWER = 0.8
@@ -119,11 +120,20 @@
     peers = others(me, n)
     lines = others(group, groups)
 
-    def only(limit, index, body, count=n):
-        if limit >= count:
-            body()
-        else:
-            pl.when(index < limit)(body)
+    first, line_first = (n - owners) // 2, (groups - tiles) // 2
+    mine, line_mine = me - first, group - line_first
+
+    def owner(body):
+        pl.when((me >= first) & (me < first + owners))(body)
+
+    def line_owner(body):
+        pl.when((group >= line_first) & (group < line_first + tiles))(body)
+
+    def other_owners(body):
+        each(0, owners, lambda o: pl.when(first + o != me)(functools.partial(body, o)))
+
+    def other_line_owners(body):
+        each(0, tiles, lambda o: pl.when(line_first + o != group)(functools.partial(body, o)))
 
     def to_peer(src, dst, send, recv, j):
         return pltpu.make_async_remote_copy(
@@ -176,13 +186,18 @@
         load.wait()
     pl.semaphore_wait(barrier, n - 1 + 3)
 
-    def part_copy(j, slot):
-        return to_peer(part_src.at[lax.rem(j, owners)], part_buf.at[slot], part_send.at[j], part_recv.at[slot], j)
+    def part_copy(o):
+        return to_peer(
+            part_src.at[o], part_buf.at[me], part_send.at[o], part_recv.at[me], first + o
+        )
+
+    def part_arrival(j):
+        return to_peer(part_src.at[0], part_buf.at[j], part_send.at[0], part_recv.at[j], j)
 
     def vec_copy(j, slot):
         return to_peer(vec_buf.at[me], vec_buf.at[slot], vec_send.at[0], vec_recv.at[0], j)
 
-    peers(lambda j: only(owners, j, lambda: part_copy(j, me).start()))
+    other_owners(lambda o: part_copy(o).start())
 
     def factor_copy(slot, i, other):
         return to_rank(factors.at[slot], factors.at[slot], fac_send.at[i], fac_recv.at[i], other)
@@ -204,37 +219,28 @@
     )
     peers(lambda j: vec_copy(j, me).start())
 
-    def own_part():
-        part_buf[me] = part_src[me]
-
-    only(owners, me, own_part)
-
+    def cross_copy(j, o):
+        return to_peer(cross.at[k, o], cross.at[k, o], cross_send.at[j], cross_recv.at[o], j)
+
+    def rank_copy(slot, i, other, j):
+        return to_rank(
+            cross.at[slot, j], cross.at[slot, j], rank_send.at[i, j], rank_recv.at[i, j], other
+        )
+
+    def pass_on(j):
+        rank_copy(k, 1, far, j).start()
+        rank_copy(k, 0, near, j).start()
+
+    @owner
     def reduce_parts():
-        peers(lambda j: part_copy(j, j).wait_recv())
+        part_buf[me] = part_src[mine]
+        peers(lambda j: part_arrival(j).wait_recv())
         total = part_buf[0].astype(F32)
         for j in range(1, n):
             total = total + part_buf[j].astype(F32)
-        cross[k, me] = total.astype(BF16)
-
-    only(owners, me, reduce_parts)
-
-    def cross_copy(j, slot):
-        return to_peer(cross.at[k, slot], cross.at[k, slot], cross_send.at[j], cross_recv.at[slot], j)
-
-    def rank_copy(slot, i, other, j):
-        return to_rank(
-            cross.at[slot, j], cross.at[slot, j], rank_send.at[i, j], rank_recv.at[i, j], other
-        )
-
-    def pass_on(j):
-        rank_copy(k, 1, far, j).start()
-        rank_copy(k, 0, near, j).start()
-
-    def send_cross():
-        peers(lambda j: cross_copy(j, me).start())
-        pass_on(me)
-
-    only(owners, me, send_cross)
+        cross[k, mine] = total.astype(BF16)
+        peers(lambda j: cross_copy(j, mine).start())
+        pass_on(mine)
 
     all_copies(vec_buf, vec_send.at[0], vec_recv.at[0]).wait_recv()
     vec = vec_buf[0]
@@ -249,11 +255,11 @@
     for i, other in enumerate((near, far, across)):
         vecs_copy(k, i, other).start()
 
-    def arrived(j):
-        cross_copy(j, j).wait_recv()
-        pass_on(j)
-
-    peers(lambda j: only(owners, j, lambda: arrived(j)), reverse=True)
+    def arrived(o):
+        cross_copy(first + o, o).wait_recv()
+        pass_on(o)
+
+    other_owners(arrived)
     factor_copy(far, 1, far).wait_recv()
     factor_copy(far, 2, near).start()
 
@@ -389,12 +395,16 @@
     u_copy.start()
     send_t((PASSES - 1) % 2, u_q, u_r)
 
-    share = prof_src.shape[1]
-
-    def prof_copy(line, slot):
-        return to_peer(
-            prof_src.at[lax.rem(line, tiles)], prof_buf.at[slot],
-            prof_send.at[line], prof_recv.at[slot], 2 * line + half,
+    def prof_copy(o, piece):
+        return to_peer(
+            prof_src.at[o, piece], prof_buf.at[group, piece],
+            prof_send.at[o, piece], prof_recv.at[group, piece], 2 * (line_first + o) + half,
+        )
+
+    def prof_arrival(line, piece):
+        return to_peer(
+            prof_src.at[0, piece], prof_buf.at[line, piece],
+            prof_send.at[0, piece], prof_recv.at[line, piece], 2 * line + half,
         )
 
     left = (krt[half].astype(F32) * u_r).astype(BF16)
@@ -406,20 +416,21 @@
     left = (mate_kern[...].astype(F32) * u_buf[1]).astype(BF16)
     total = total + dot(left, mate_expr[...])
     prof_src[...] = total.astype(BF16).reshape(prof_src.shape)
-    lines(lambda line: only(tiles, line, lambda: prof_copy(line, group).start(), groups))
-
+    for piece in range(HALVES):
+        other_line_owners(lambda o: prof_copy(o, piece).start())
+
+    @line_owner
     def own_prof():
-        prof_buf[group] = prof_src[group]
-
-    only(tiles, group, own_prof, groups)
+        prof_buf[group] = prof_src[line_mine]
 
     v, weights, t = new_weights((PASSES - 1) % 2, v)
 
-    def sends(j):
-        only(owners, j, lambda: part_copy(j, j).wait_send())
-        only(owners, me, lambda: cross_copy(j, me).wait_send())
-
-    peers(sends)
+    other_owners(lambda o: part_copy(o).wait_send())
+
+    @owner
+    def cross_sends():
+        peers(lambda j: cross_copy(j, mine).wait_send())
+
     all_copies(vec_buf, vec_send.at[0], vec_recv.at[0]).wait_send()
     all_copies(peaks, peak_send.at[0], peak_recv.at[0]).wait_send()
     for i, (slot, other) in enumerate(((k, near), (k, far), (far, near))):
@@ -462,35 +473,38 @@
         columns = slice(i * width, (i + 1) * width)
         scaled[i] = (kq[:, columns].astype(F32) * ratio[:, columns]).astype(BF16)
 
-    def gather_copy(line, slot):
-        return to_peer(
-            prof.at[half, slot], prof.at[half, slot],
-            gat_send.at[line], gat_recv.at[slot], 2 * line + half,
-        )
-
-    def forward_copy(side, slot):
-        return to_peer(
-            prof.at[side, slot], prof.at[side, slot], fwd_send.at[slot], fwd_recv.at[slot], mate
-        )
-
+    def gather_copy(line, o, piece):
+        return to_peer(
+            prof.at[half, o, piece], prof.at[half, o, piece],
+            gat_send.at[line, piece], gat_recv.at[o, piece], 2 * line + half,
+        )
+
+    def forward_copy(side, o, piece):
+        return to_peer(
+            prof.at[side, o, piece], prof.at[side, o, piece],
+            fwd_send.at[o, piece], fwd_recv.at[o, piece], mate,
+        )
+
+    @line_owner
     def reduce_prof():
-        lines(lambda line: prof_copy(line, line).wait_recv())
-        total = prof_buf[0].astype(F32)
-        for line in range(1, groups):
-            total = total + prof_buf[line].astype(F32)
-        prof[half, group] = total.astype(BF16)
-        lines(lambda line: gather_copy(line, group).start())
-        forward_copy(half, group).start()
-
-    only(tiles, group, reduce_prof, groups)
-
-    def gathered(line):
-        gather_copy(line, line).wait_recv()
-        forward_copy(half, line).start()
-
-    lines(lambda line: only(tiles, line, lambda: gathered(line), groups), reverse=True)
-    flat = (tiles * share, prof.shape[3])
-    each(0, tiles, lambda line: forward_copy(1 - half, line).wait_recv())
+        for piece in range(HALVES):
+            lines(lambda line: prof_arrival(line, piece).wait_recv())
+            total = prof_buf[0, piece].astype(F32)
+            for line in range(1, groups):
+                total = total + prof_buf[line, piece].astype(F32)
+            prof[half, line_mine, piece] = total.astype(BF16)
+            lines(lambda line: gather_copy(line, line_mine, piece).start())
+            forward_copy(half, line_mine, piece).start()
+
+    def gathered(o, piece):
+        gather_copy(line_first + o, o, piece).wait_recv()
+        forward_copy(half, o, piece).start()
+
+    for piece in range(HALVES):
+        other_line_owners(lambda o: gathered(o, piece))
+    flat = (scaled.shape[2], prof.shape[4])
+    for piece in range(HALVES):
+        each(0, tiles, lambda o: forward_copy(1 - half, o, piece).wait_recv())
     for i in range(BLOCKS):
         rows = block_rows(i)
         mixed = dot(scaled[half, rows], prof[half].reshape(flat))
@@ -499,12 +513,15 @@
         pred_out[rows] = (mixed * across_genes).astype(BF16)
         stores[3 + i].start()
 
-    def last_sends(line):
-        only(tiles, group, lambda: gather_copy(line, group).wait_send(), groups)
-
-    lines(last_sends)
-    lines(lambda line: only(tiles, line, lambda: prof_copy(line, line).wait_send(), groups))
-    each(0, tiles, lambda line: forward_copy(half, line).wait_send())
+    for piece in range(HALVES):
+        other_line_owners(lambda o: prof_copy(o, piece).wait_send())
+        each(0, tiles, lambda o: forward_copy(half, o, piece).wait_send())
+
+    @line_owner
+    def gather_sends():
+        for piece in range(HALVES):
+            lines(lambda line: gather_copy(line, line_mine, piece).wait_send())
+
     for store in stores:
         store.wait()
 
@@ -538,16 +555,16 @@
     rows, dim = x_emb.shape
     genes = expr.shape[1]
     rank_all = ranks * LANES
-    owners = min(n, dim // 16)
+    owners = min(n // 2, dim // 16)
     groups = n // 2
-    tiles = min(groups, rank_all // 2 // 16)
+    tiles = min(groups // 2, rank_all // 2 // (16 * HALVES))
     hbm = pl.BlockSpec(memory_space=pltpu.HBM)
     dma = pltpu.SemaphoreType.DMA
     pair = [dma((n,)), dma((n,))]
     single = [dma((1,)), dma((1,))]
     three = [dma((3,)), dma((3,))]
-    lined = [dma((groups,)), dma((groups,))]
-    block = (rank_all // 2 // tiles, genes)
+    lined = [dma((groups, HALVES)), dma((groups, HALVES))]
+    block = (HALVES, rank_all // 2 // tiles // HALVES, genes)
     shapes = (
         jax.ShapeDtypeStruct(q_factor.shape, F32),
         jax.ShapeDtypeStruct(r_factor.shape, F32),

time: 88.1 us -> 88.1 us (level)
  no operation moved by 1% of the time
where the time goes in v5:
time: 88.1 us; the launch traced here: 87.9 us
  Pallas kernels  87.3 us (99%)
    pallas_call x1, Pallas kernels, shards(): pl.pallas_call(functools.partial(kernel, n, ranks, owners, tiles, float(r...  85.1 us
    pallas_call x1, Pallas kernels, shards(): pl.pallas_call(functools.partial(write_out, len(shapes)), out_shape=shape...  2.24 us

profile of v5, /device:TPU:0, one launch (start us, length us, event | category | flops | bytes accessed | tf_op | source)
XLA Modules:
  0.0 87.9 jit_solution(15966378481296143804)
XLA Ops:
  0.6 85.1 %transport_step.1 = (f32[512,128]{1,0:T(8,128)}, f32[512,128]{1,0:T(8,128)}, f32[1,128]{1,0:T(1,128)}, bf16[512,512]{1,0:T(8,128)(2,1)}) custom-call(bf16[512,256]{1,0:T(8,128)(2,1)} %x_hbm.1, bf16[512,256]{1,0:T(8,128)(2,1)} %y_hbm.1, f32[512,128]{1,0:T(8,128)} %q_hbm.1, f32[512,128]{1,0:T(8,128)} %r_hbm.1, f32[1,128]{1,0:T(1,128)} %bitcast.6, ...), custom_call_target="tpu_custom_call" | custom-call | flops 872415232 | bytes 4194304 | tf_op jit(solution)/shard_map/transport_step/pallas_call | solution.py:574
  85.7 2.2 %write_out.1 = (f32[512,128]{1,0:T(8,128)}, f32[512,128]{1,0:T(8,128)}, f32[1,128]{1,0:T(1,128)}, bf16[512,512]{1,0:T(8,128)(2,1)}) custom-call(f32[512,128]{1,0:T(8,128)} %get-tuple-element.12.refs_0_, f32[512,128]{1,0:T(8,128)} %get-tuple-element.13.refs_1_, f32[1,128]{1,0:T(1,128)} %get-tuple-element.14.refs_2_, bf16[512,512]{1,0:T(8,128)(2,1)} %get-tuple-element.15.refs_3_), custom_call_target="tpu_custom_call" | custom-call | tf_op jit(solution)/shard_map/write_out/pallas_call | solution.py:636

commit v6 on v5

--- a/solution.py
+++ b/solution.py
@@ -72,7 +72,7 @@
     q_out, r_out, w_out, pred_out, out_sem,
     x_ref, y_ref, q_ref, r_ref, g_ref, a_ref, b_ref, expr_ref, in_sem,
     factors, part_src, part_buf, cross, vec_buf, vecs, grads_q, grads_r, grads_g,
-    peaks, kq, kr, kqt, krt, t_buf, mate_kern, mate_expr, u_buf, scaled,
+    factors_t, grads_t, peaks, kq, kr, kqt, krt, t_buf, mate_kern, mate_expr, u_buf, scaled,
     prof_src, prof_buf, prof,
     part_send, part_recv, vec_send, vec_recv, cross_send, cross_recv,
     fac_send, fac_recv, rank_send, rank_recv, vr_send, vr_recv,
@@ -151,6 +151,11 @@
         most = slots.at[pl.ds(0, n - 1)]
         return to_peer(most, most, send, recv, mate)
 
+    barrier = pltpu.get_barrier_semaphore()
+    peers(lambda j: pl.semaphore_signal(barrier, inc=1, device_id=(j, k), device_id_type=MESH))
+    for other in (near, far, across):
+        pl.semaphore_signal(barrier, inc=1, device_id=(me, other), device_id_type=MESH)
+
     loads = [
         pltpu.make_async_copy(src, dst, in_sem.at[i])
         for i, (src, dst) in enumerate(
@@ -162,10 +167,6 @@
     ]
     for load in loads:
         load.start()
-    barrier = pltpu.get_barrier_semaphore()
-    peers(lambda j: pl.semaphore_signal(barrier, inc=1, device_id=(j, k), device_id_type=MESH))
-    for other in (near, far, across):
-        pl.semaphore_signal(barrier, inc=1, device_id=(me, other), device_id_type=MESH)
 
     depth = part_src.shape[2]
     loads[0].wait()
@@ -324,6 +325,11 @@
     factor_copy(near, 0, near).wait_recv()
     factor_copy(across, 2, near).wait_recv()
     log_a, log_b = jnp.log(a_ref[...]), jnp.log(b_ref[...])
+    for kk in range(ranks):
+        grads_t[kk, 0] = jnp.transpose(grads_q[kk])
+        grads_t[kk, 1] = jnp.transpose(grads_r[kk])
+        factors_t[kk, 0] = jnp.transpose(factors[kk, 0])
+        factors_t[kk, 1] = jnp.transpose(factors[kk, 1])
     all_copies(peaks, peak_send.at[0], peak_recv.at[0]).wait_recv()
     top = peaks[0]
     for j in range(1, n):
@@ -335,12 +341,14 @@
         columns = slice(kk * LANES, (kk + 1) * LANES)
         kern_q = factors[kk, 0].astype(F32) * jnp.exp(-eta * grads_q[kk])
         kern_r = factors[kk, 1].astype(F32) * jnp.exp(-eta * grads_r[kk])
-        kern_q, kern_r = kern_q.astype(BF16), kern_r.astype(BF16)
-        kq[:, columns] = kern_q
-        kr[:, columns] = kern_r
-        kqt[columns, :] = jnp.transpose(kern_q)
+        kq[:, columns] = kern_q.astype(BF16)
+        kr[:, columns] = kern_r.astype(BF16)
+        kern_qt, kern_rt = (
+            factors_t[kk, i].astype(F32) * jnp.exp(-eta * grads_t[kk, i]) for i in range(2)
+        )
+        kqt[columns, :] = kern_qt.astype(BF16)
         rows = slice(kk % 2 * LANES, (kk % 2 + 1) * LANES)
-        krt[kk // 2, rows, :] = jnp.transpose(kern_r)
+        krt[kk // 2, rows, :] = kern_rt.astype(BF16)
         log_g.append(jnp.log(vecs[kk][4:5]) - eta * grads_g[kk][0:1])
     log_kern_g = jnp.concatenate(log_g + log_g, axis=0)
 
@@ -353,11 +361,9 @@
     def t_all(parity):
         return all_copies(t_buf.at[parity], t_send.at[parity], t_recv.at[parity])
 
-    def whole_krt():
-        return krt[...].reshape(ranks * LANES, krt.shape[2])
-
     def marginals(v):
-        s_r = row_product(wide(v, ranks, ranks), whole_krt())
+        s_r = row_product(wide(v, ranks, ranks // 2), krt[0])
+        s_r = s_r + row_product(wide(v, ranks + ranks // 2, ranks // 2), krt[1])
         u_r = jnp.exp(POWER * (log_b - jnp.log(s_r)))
         s_q = row_product(wide(v, 0, ranks), kqt[...])
         u_q = jnp.exp(POWER * (log_a - jnp.log(s_q)))
@@ -600,6 +606,8 @@
             pltpu.VMEM((ranks, rows, LANES), F32),
             pltpu.VMEM((ranks, rows, LANES), F32),
             pltpu.VMEM((ranks, 8, LANES), F32),
+            pltpu.VMEM((ranks, 2, LANES, rows), BF16),
+            pltpu.VMEM((ranks, 2, LANES, rows), F32),
             pltpu.VMEM((n, 8, LANES), F32),
             pltpu.VMEM((rows, rank_all), BF16),
             pltpu.VMEM((rows, rank_all), BF16),

time: 88.1 us -> 88.5 us (level)
  no operation moved by 1% of the time
where the time goes in v6:
time: 88.5 us; the launch traced here: 88.4 us
  Pallas kernels  87.7 us (99%)
    pallas_call x1, Pallas kernels, shards(): pl.pallas_call(functools.partial(kernel, n, ranks, owners, tiles, float(r...  85.5 us
    pallas_call x1, Pallas kernels, shards(): pl.pallas_call(functools.partial(write_out, len(shapes)), out_shape=shape...  2.24 us

profile of v6, /device:TPU:0, one launch (start us, length us, event | category | flops | bytes accessed | tf_op | source)
XLA Modules:
  0.0 88.4 jit_solution(9782692939928654968)
XLA Ops:
  0.6 85.5 %transport_step.1 = (f32[512,128]{1,0:T(8,128)}, f32[512,128]{1,0:T(8,128)}, f32[1,128]{1,0:T(1,128)}, bf16[512,512]{1,0:T(8,128)(2,1)}) custom-call(bf16[512,256]{1,0:T(8,128)(2,1)} %x_hbm.1, bf16[512,256]{1,0:T(8,128)(2,1)} %y_hbm.1, f32[512,128]{1,0:T(8,128)} %q_hbm.1, f32[512,128]{1,0:T(8,128)} %r_hbm.1, f32[1,128]{1,0:T(1,128)} %bitcast.6, ...), custom_call_target="tpu_custom_call" | custom-call | flops 872415232 | bytes 4194304 | tf_op jit(solution)/shard_map/transport_step/pallas_call | solution.py:580
  86.1 2.2 %write_out.1 = (f32[512,128]{1,0:T(8,128)}, f32[512,128]{1,0:T(8,128)}, f32[1,128]{1,0:T(1,128)}, bf16[512,512]{1,0:T(8,128)(2,1)}) custom-call(f32[512,128]{1,0:T(8,128)} %get-tuple-element.12.refs_0_, f32[512,128]{1,0:T(8,128)} %get-tuple-element.13.refs_1_, f32[1,128]{1,0:T(1,128)} %get-tuple-element.14.refs_2_, bf16[512,512]{1,0:T(8,128)(2,1)} %get-tuple-element.15.refs_3_), custom_call_target="tpu_custom_call" | custom-call | tf_op jit(solution)/shard_map/write_out/pallas_call | solution.py:644

commit v7 on v5

--- a/solution.py
+++ b/solution.py
@@ -151,6 +151,11 @@
         most = slots.at[pl.ds(0, n - 1)]
         return to_peer(most, most, send, recv, mate)
 
+    barrier = pltpu.get_barrier_semaphore()
+    peers(lambda j: pl.semaphore_signal(barrier, inc=1, device_id=(j, k), device_id_type=MESH))
+    for other in (near, far, across):
+        pl.semaphore_signal(barrier, inc=1, device_id=(me, other), device_id_type=MESH)
+
     loads = [
         pltpu.make_async_copy(src, dst, in_sem.at[i])
         for i, (src, dst) in enumerate(
@@ -162,11 +167,6 @@
     ]
     for load in loads:
         load.start()
-    barrier = pltpu.get_barrier_semaphore()
-    peers(lambda j: pl.semaphore_signal(barrier, inc=1, device_id=(j, k), device_id_type=MESH))
-    for other in (near, far, across):
-        pl.semaphore_signal(barrier, inc=1, device_id=(me, other), device_id_type=MESH)
-
     depth = part_src.shape[2]
     loads[0].wait()
     q = q_ref[...]
@@ -228,6 +228,7 @@
         )
 
     def pass_on(j):
+        rank_copy(k, 2, across, j).start()
         rank_copy(k, 1, far, j).start()
         rank_copy(k, 0, near, j).start()
 
@@ -304,16 +305,11 @@
     vecs_copy(near, 0, near).wait_recv()
     each(0, owners, lambda j: rank_copy(near, 0, near, j).wait_recv())
     peak = jnp.maximum(peak, gradients(near))
-
-    def across_x(j):
-        rank_copy(far, 1, far, j).wait_recv()
-        rank_copy(far, 2, near, j).start()
-
-    each(0, owners, across_x)
+    each(0, owners, lambda j: rank_copy(far, 1, far, j).wait_recv())
     vecs_copy(far, 1, far).wait_recv()
     peak = jnp.maximum(peak, gradients(far))
     vecs_copy(across, 2, across).wait_recv()
-    each(0, owners, lambda j: rank_copy(across, 2, near, j).wait_recv())
+    each(0, owners, lambda j: rank_copy(across, 2, across, j).wait_recv())
     peak = jnp.maximum(peak, gradients(across))
     peaks[me] = jnp.broadcast_to(peak, (8, LANES))
 
@@ -435,8 +431,8 @@
     all_copies(peaks, peak_send.at[0], peak_recv.at[0]).wait_send()
     for i, (slot, other) in enumerate(((k, near), (k, far), (far, near))):
         factor_copy(slot, i, other).wait_send()
-        each(0, owners, lambda j: rank_copy(slot, i, other, j).wait_send())
     for i, other in enumerate((near, far, across)):
+        each(0, owners, lambda j: rank_copy(k, i, other, j).wait_send())
         vecs_copy(k, i, other).wait_send()
     u_copy.wait_send()
     for piece in range(PIECES):

time: 88.1 us -> 89.3 us (1.014)
  Pallas kernels: 87.3 us -> 88.5 us
    pallas_call x1, Pallas kernels: 85.1 us -> 86.2 us  [shards(): pl.pallas_call(functools.partial(kernel, n, ranks, owners, tiles, float(r...]
where the time goes in v7:
time: 89.3 us; the launch traced here: 89.1 us
  Pallas kernels  88.5 us (99%)
    pallas_call x1, Pallas kernels, shards(): pl.pallas_call(functools.partial(kernel, n, ranks, owners, tiles, float(r...  86.2 us
    pallas_call x1, Pallas kernels, shards(): pl.pallas_call(functools.partial(write_out, len(shapes)), out_shape=shape...  2.24 us

profile of v7, /device:TPU:0, one launch (start us, length us, event | category | flops | bytes accessed | tf_op | source)
XLA Modules:
  0.0 89.1 jit_solution(8925705692765686841)
XLA Ops:
  0.6 86.2 %transport_step.1 = (f32[512,128]{1,0:T(8,128)}, f32[512,128]{1,0:T(8,128)}, f32[1,128]{1,0:T(1,128)}, bf16[512,512]{1,0:T(8,128)(2,1)}) custom-call(bf16[512,256]{1,0:T(8,128)(2,1)} %x_hbm.1, bf16[512,256]{1,0:T(8,128)(2,1)} %y_hbm.1, f32[512,128]{1,0:T(8,128)} %q_hbm.1, f32[512,128]{1,0:T(8,128)} %r_hbm.1, f32[1,128]{1,0:T(1,128)} %bitcast.6, ...), custom_call_target="tpu_custom_call" | custom-call | flops 872415232 | bytes 4194304 | tf_op jit(solution)/shard_map/transport_step/pallas_call | solution.py:570
  86.9 2.2 %write_out.1 = (f32[512,128]{1,0:T(8,128)}, f32[512,128]{1,0:T(8,128)}, f32[1,128]{1,0:T(1,128)}, bf16[512,512]{1,0:T(8,128)(2,1)}) custom-call(f32[512,128]{1,0:T(8,128)} %get-tuple-element.12.refs_0_, f32[512,128]{1,0:T(8,128)} %get-tuple-element.13.refs_1_, f32[1,128]{1,0:T(1,128)} %get-tuple-element.14.refs_2_, bf16[512,512]{1,0:T(8,128)(2,1)} %get-tuple-element.15.refs_3_), custom_call_target="tpu_custom_call" | custom-call | tf_op jit(solution)/shard_map/write_out/pallas_call | solution.py:632
